TPU v7x, 128 devices: a whole 4x4x4 slice. The times are simulated.
128 devices in a mesh: blk: 16 (over z_hi, x, core), uly: 8 (over y, z_lo).
Axes of the slice: x: 4, y: 4, z: 4 (z_hi: 2, z_lo: 2; z = z_hi * 2 + z_lo), core: 2. Of those that a mesh axis runs over, the one named last changes fastest.
Arguments:
- queries: bfloat16 [16384, 4096], P(('blk', 'uly')), may hold values from -6 to 6
- input_keys: bfloat16 [16384, 1024], P(('blk', 'uly')), may hold values from -6 to 6
- input_values: bfloat16 [16384, 1024], P(('blk', 'uly')), may hold values from -6 to 6
- outputs: bfloat16 [16384, 4096], P(('blk', 'uly')), may hold values from -2 to 2
- output_gradient: bfloat16 [16384, 4096], P(('blk', 'uly')), may hold values from -6 to 6
- saved_logsumexp: float32 [16384, 32], P(('blk', 'uly')), may hold values from -0.5 to 12
- span_order: int32 [16, 2], replicated, may hold values from 0 to 31, as said below
Outputs:
- grad_queries: bfloat16 [16384, 4096], P(('blk', 'uly'))
- key_gradient: bfloat16 [16384, 1024], P(('blk', 'uly'))
- value_gradient: bfloat16 [16384, 1024], P(('blk', 'uly'))
Inputs may be any that keep to these rules, and one draw needn't show every extreme that they name: `span_order`: row r names two position blocks c and 31 - c for some c, in either order; every block of 0 to 31 appears exactly once in the table.
All inputs are finite; a program needn't handle non-finite values.
Results may differ from a plain program's by a relative error of at most 0.005.
Values may be sent and summed in bfloat16 or wider, within the bound.
No kernel may reach another device: no remote copies, remote signals or barrier semaphores. Data moves between devices by JAX's collectives and lax.ppermute only.
A program may use at most 128 MiB of HBM per device.

v0:
```python
import math

import jax
import jax.numpy as jnp
from jax import lax
from jax.sharding import PartitionSpec as P

HEAD_DIMENSION = 128


def from_behind(value, axis, by):
    length = lax.axis_size(axis)
    return lax.ppermute(value, axis, [(i, (i + by) % length) for i in range(length)])


def layout_positions(order_table, cycle_slot, row_count):
    half_rows = row_count // 2
    offsets = jnp.arange(row_count, dtype=jnp.int32)
    pair = lax.dynamic_index_in_dim(order_table, cycle_slot, 0, keepdims=False)
    lower = pair[0] * half_rows + offsets
    upper = pair[1] * half_rows + offsets - half_rows
    return jnp.where(offsets < half_rows, lower, upper)


def row_deltas(output_gradient, outputs, head_size):
    row_count = output_gradient.shape[0]
    product = output_gradient.astype(jnp.float32) * outputs.astype(jnp.float32)
    return product.reshape(row_count, -1, head_size).sum(axis=2)


def tile_grads(query_side, query_pos, key_side, key_pos, head_size):
    queries, output_gradient, saved_logsumexp, row_delta_values = query_side
    key_block, value_block = key_side
    query_count = queries.shape[0]
    key_count = key_block.shape[0]
    kv_heads = key_block.shape[1] // head_size
    query_groups = queries.shape[1] // head_size // kv_heads
    factor = 1.0 / math.sqrt(head_size)
    query_per_head = queries.reshape(query_count, kv_heads, query_groups, head_size)
    gradient_per_head = output_gradient.reshape(query_count, kv_heads, query_groups, head_size)
    key_per_head = key_block.reshape(key_count, kv_heads, head_size)
    value_per_head = value_block.reshape(key_count, kv_heads, head_size)
    scores = jnp.einsum(
        "rkgd,ckd->kgrc", query_per_head, key_per_head, preferred_element_type=jnp.float32
    )
    stat_cols = saved_logsumexp.reshape(query_count, kv_heads, query_groups).transpose(1, 2, 0)[
        ..., None
    ]
    delta_cols = row_delta_values.reshape(query_count, kv_heads, query_groups).transpose(1, 2, 0)[
        ..., None
    ]
    visible = (query_pos[:, None] >= key_pos[None, :])[None, None, :, :]
    probs = jnp.where(visible, jnp.exp(scores * factor - stat_cols), 0.0)
    probs_low = probs.astype(jnp.bfloat16)
    d_probs = jnp.einsum(
        "rkgd,ckd->kgrc", gradient_per_head, value_per_head, preferred_element_type=jnp.float32
    )
    d_scores = (probs * (d_probs - delta_cols) * factor).astype(jnp.bfloat16)
    value_gradient = jnp.einsum(
        "kgrc,rkgd->ckd", probs_low, gradient_per_head, preferred_element_type=jnp.float32
    )
    key_gradient = jnp.einsum(
        "kgrc,rkgd->ckd", d_scores, query_per_head, preferred_element_type=jnp.float32
    )
    grad_queries = jnp.einsum(
        "kgrc,ckd->rkgd", d_scores, key_per_head, preferred_element_type=jnp.float32
    )
    return (
        grad_queries.reshape(query_count, -1),
        key_gradient.reshape(key_count, -1),
        value_gradient.reshape(key_count, -1),
    )


def pair_grads(query_side, query_slot, key_side, key_slot, order_table, head_size):
    row_count = query_side[0].shape[0]
    query_pos = layout_positions(order_table, query_slot, row_count)
    key_pos = layout_positions(order_table, key_slot, row_count)
    return tile_grads(query_side, query_pos, key_side, key_pos, head_size)


def body(queries, input_keys, input_values, outputs, output_gradient, saved_logsumexp, span_order):
    head_size = HEAD_DIMENSION
    queries, input_keys, input_values, outputs, output_gradient = (
        lax.all_to_all(queries, "uly", split_axis=1, concat_axis=0, tiled=True),
        lax.all_to_all(input_keys, "uly", split_axis=1, concat_axis=0, tiled=True),
        lax.all_to_all(input_values, "uly", split_axis=1, concat_axis=0, tiled=True),
        lax.all_to_all(outputs, "uly", split_axis=1, concat_axis=0, tiled=True),
        lax.all_to_all(output_gradient, "uly", split_axis=1, concat_axis=0, tiled=True),
    )
    saved_logsumexp = lax.all_to_all(
        saved_logsumexp, "uly", split_axis=1, concat_axis=0, tiled=True
    )
    row_delta_values = row_deltas(output_gradient, outputs, head_size)
    cycle_size = lax.axis_size("blk")
    cycle_slot = lax.axis_index("blk")
    query_side = (queries, output_gradient, saved_logsumexp, row_delta_values)
    local = pair_grads(
        query_side, cycle_slot, (input_keys, input_values), cycle_slot, span_order, head_size
    )
    prev_slot = (cycle_slot + cycle_size - 1) % cycle_size
    moving_keys, moving_values = from_behind((input_keys, input_values), "blk", 1)
    cross = pair_grads(
        query_side, cycle_slot, (moving_keys, moving_values), prev_slot, span_order, head_size
    )
    returned_keys, returned_values = from_behind((cross[1], cross[2]), "blk", -1)
    grad_queries = local[0] + cross[0]
    key_gradient = local[1] + returned_keys
    value_gradient = local[2] + returned_values
    grad_queries = grad_queries.astype(jnp.bfloat16)
    key_gradient = key_gradient.astype(jnp.bfloat16)
    value_gradient = value_gradient.astype(jnp.bfloat16)
    grad_queries, key_gradient, value_gradient = (
        lax.all_to_all(grad_queries, "uly", split_axis=0, concat_axis=1, tiled=True),
        lax.all_to_all(key_gradient, "uly", split_axis=0, concat_axis=1, tiled=True),
        lax.all_to_all(value_gradient, "uly", split_axis=0, concat_axis=1, tiled=True),
    )
    return (grad_queries, key_gradient, value_gradient)


def solution(mesh):
    in_specs = (
        P(("blk", "uly"), None),
        P(("blk", "uly"), None),
        P(("blk", "uly"), None),
        P(("blk", "uly"), None),
        P(("blk", "uly"), None),
        P(("blk", "uly"), None),
        P(),
    )
    out_specs = (P(("blk", "uly"), None), P(("blk", "uly"), None), P(("blk", "uly"), None))
    return jax.shard_map(body, mesh=mesh, in_specs=in_specs, out_specs=out_specs, check_vma=False)
```

profile of v0, /device:TPU:64, one launch (start us, length us, event | category | flops | bytes accessed | tf_op | source)
XLA Modules:
  0.0 194.1 jit_solution(16744672568197277437)
XLA Ops:
  2.3 5.5 %all-to-all-start = ((bf16[128,8,128]{2,0,1:T(8,128)(2,1)}), bf16[128,8,128]{2,0,1:T(8,128)(2,1)S(1)}, u32[]{:S(2)}, u32[]{:S(2)}) async-start(bf16[128,8,128]{2,0,1:T(8,128)(2,1)} %copy_bitcast_fusion.3), calls=%async_computation | async-start | bytes 524288 | tf_op jit(solution)/shard_map/all_to_all | solution.py:86
  7.9 1.7 copy_bitcast_fusion.2
  9.6 5.5 %all-to-all-done = bf16[128,8,128]{2,0,1:T(8,128)(2,1)S(1)} async-done(((bf16[128,8,128]{2,0,1:T(8,128)(2,1)}), bf16[128,8,128]{2,0,1:T(8,128)(2,1)S(1)}, u32[]{:S(2)}, u32[]{:S(2)}) %all-to-all-start) | async-done | bytes 262176 | tf_op jit(solution)/shard_map/all_to_all | solution.py:86
  15.1 4.1 %all-to-all-start.3 = ((bf16[128,8,128]{2,0,1:T(8,128)(2,1)}), bf16[128,8,128]{2,0,1:T(8,128)(2,1)}, u32[]{:S(2)}, u32[]{:S(2)}) async-start(bf16[128,8,128]{2,0,1:T(8,128)(2,1)} %copy_bitcast_fusion.2), calls=%async_computation.3 | async-start | bytes 524288 | tf_op jit(solution)/shard_map/all_to_all | solution.py:87
  19.1 2.3 %copy.55 = bf16[128,4096]{0,1:T(8,128)(2,1)} copy(bf16[128,4096]{1,0:T(8,128)(2,1)} %param.7) | data formatting | bytes 2097152 | tf_op args[0]
  21.4 4.7 %all-to-all-done.3 = bf16[128,8,128]{2,0,1:T(8,128)(2,1)} async-done(((bf16[128,8,128]{2,0,1:T(8,128)(2,1)}), bf16[128,8,128]{2,0,1:T(8,128)(2,1)}, u32[]{:S(2)}, u32[]{:S(2)}) %all-to-all-start.3) | async-done | bytes 262176 | tf_op jit(solution)/shard_map/all_to_all | solution.py:87
  26.1 3.6 %all-to-all-start.1 = ((bf16[128,8,512]{0,2,1:T(8,128)(2,1)}), bf16[128,8,512]{0,2,1:T(8,128)(2,1)S(1)}, u32[]{:S(2)}, u32[]{:S(2)}) async-start(bf16[128,8,512]{0,2,1:T(8,128)(2,1)} %bitcast.5), calls=%async_computation.1 | async-start | bytes 2097152 | tf_op jit(solution)/shard_map/all_to_all | solution.py:85
  29.7 2.3 %copy.59 = bf16[128,4096]{0,1:T(8,128)(2,1)} copy(bf16[128,4096]{1,0:T(8,128)(2,1)} %param.11) | data formatting | bytes 2097152 | tf_op args[4]
  31.9 10.9 %all-to-all-done.1 = bf16[128,8,512]{0,2,1:T(8,128)(2,1)S(1)} async-done(((bf16[128,8,512]{0,2,1:T(8,128)(2,1)}), bf16[128,8,512]{0,2,1:T(8,128)(2,1)S(1)}, u32[]{:S(2)}, u32[]{:S(2)}) %all-to-all-start.1) | async-done | bytes 1048608 | tf_op jit(solution)/shard_map/all_to_all | solution.py:85
  42.8 3.6 %all-to-all-start.4 = ((bf16[128,8,512]{0,2,1:T(8,128)(2,1)}), bf16[128,8,512]{0,2,1:T(8,128)(2,1)S(1)}, u32[]{:S(2)}, u32[]{:S(2)}) async-start(bf16[128,8,512]{0,2,1:T(8,128)(2,1)} %bitcast.17), calls=%async_computation.4 | async-start | bytes 2097152 | tf_op jit(solution)/shard_map/all_to_all | solution.py:89
  50.3 2.3 %copy.62 = bf16[128,4096]{0,1:T(8,128)(2,1)} copy(bf16[128,4096]{1,0:T(8,128)(2,1)} %param.10) | data formatting | bytes 2097152 | tf_op args[3]
  52.7 2.3 %broadcast_compare_fusion = (pred[1024,1024]{0,1:T(8,128)(4,1)}, pred[1024,1024]{0,1:T(8,128)(4,1)}) fusion(s32[1024]{0:T(1024)S(1)} %add_select_fusion.1, s32[1024]{0:T(1024)S(1)} %add_select_fusion), kind=kLoop, calls=%fused_computation.33 | loop fusion | flops 2097152 | bytes 2105344 | tf_op jit(solution)/shard_map/ge | solution.py:52
  55.0 1.6 collective-permute-start.1
  57.7 3.5 %all-to-all-done.4 = bf16[128,8,512]{0,2,1:T(8,128)(2,1)S(1)} async-done(((bf16[128,8,512]{0,2,1:T(8,128)(2,1)}), bf16[128,8,512]{0,2,1:T(8,128)(2,1)S(1)}, u32[]{:S(2)}, u32[]{:S(2)}) %all-to-all-start.4) | async-done | bytes 1048608 | tf_op jit(solution)/shard_map/all_to_all | solution.py:89
  61.2 7.4 %all-to-all-start.2 = ((f32[128,8,4]{0,2,1:T(4,128)}), f32[128,8,4]{0,2,1:T(4,128)S(1)}, u32[]{:S(2)}, u32[]{:S(2)}) async-start(f32[128,8,4]{0,2,1:T(4,128)} %bitcast.9), calls=%async_computation.2 | async-start | bytes 32768 | tf_op jit(solution)/shard_map/all_to_all | solution.py:91
  68.7 9.0 %fusion.59 = f32[1024,1024,4]{1,0,2:T(8,128)} fusion(bf16[1024,4,128]{0,2,1:T(8,128)(2,1)S(1)} %reshape.246, bf16[1024,128]{1,0:T(8,128)(2,1)} %collective-permute-done), kind=kOutput, calls=%fused_computation.50 | convolution fusion | flops 1073741824 | bytes 18087936 | tf_op jit(solution)/shard_map/rkgd,ckd->kgrc/dot_general | solution.py:43
  78.9 5.7 %all-to-all-start.5 = ((bf16[128,8,512]{0,2,1:T(8,128)(2,1)}), bf16[128,8,512]{0,2,1:T(8,128)(2,1)S(1)}, u32[]{:S(2)}, u32[]{:S(2)}) async-start(bf16[128,8,512]{0,2,1:T(8,128)(2,1)} %bitcast.210), calls=%async_computation.5 | async-start | bytes 2097152 | tf_op jit(solution)/shard_map/all_to_all | solution.py:88
  84.6 8.4 %fusion.39 = f32[1024,128]{1,0:T(8,128)} fusion(bf16[1024,4,128]{0,2,1:T(8,128)(2,1)S(1)} %reshape.249, f32[1024,1024,4]{1,0,2:T(8,128)} %fusion.59, f32[4,1024]{1,0:T(4,128)S(1)} %bitcast.219, pred[1024,1024]{0,1:T(8,128)(4,1)} %get-tuple-element.9), kind=kOutput, calls=%fused_computation.38 | convolution fusion | flops 1090519040 | bytes 19415040 | tf_op jit(solution)/shard_map/kgrc,rkgd->ckd/dot_general | solution.py:59
  93.0 6.9 %all-to-all-done.5 = bf16[128,8,512]{0,2,1:T(8,128)(2,1)S(1)} async-done(((bf16[128,8,512]{0,2,1:T(8,128)(2,1)}), bf16[128,8,512]{0,2,1:T(8,128)(2,1)S(1)}, u32[]{:S(2)}, u32[]{:S(2)}) %all-to-all-start.5) | async-done | bytes 1048608 | tf_op jit(solution)/shard_map/all_to_all | solution.py:88
  102.8 2.2 %multiply_reduce_fusion = f32[1024,4]{0,1:T(4,128)S(1)} fusion(f32[1024,4,128]{0,2,1:T(8,128)} %reshape.255, bf16[1024,4,128]{0,2,1:T(8,128)(2,1)} %copy-done.4), kind=kLoop, calls=%fused_computation.32 | loop fusion | flops 1568768 | bytes 3162112 | tf_op jit(solution)/shard_map/reduce_sum | solution.py:28
  105.0 12.2 %fusion.2 = bf16[1,4,1024,1024]{2,3,1,0:T(8,128)(2,1)S(1)} fusion(f32[1024,1024,4]{1,0,2:T(8,128)} %fusion.59, bf16[1024,4,128]{0,2,1:T(8,128)(2,1)} %copy-done.4, f32[4,1024]{1,0:T(4,128)S(1)} %bitcast.217, f32[4,1024]{1,0:T(4,128)S(1)} %bitcast.220, pred[1024,1024]{0,1:T(8,128)(4,1)} %get-tuple-element.9, bf16[1024,128]{1,0:T(8,128)(2,1)} %collective-permute-done.1), kind=kOutput, calls=%fused_computation.3 | convolution fusion | flops 1103101952 | bytes 27557888 | tf_op jit(solution)/shard_map/rkgd,ckd->kgrc/dot_general | solution.py:55
  117.2 3.5 %fusion.36 = f32[1024,128]{1,0:T(8,128)} fusion(bf16[1024,4,128]{0,2,1:T(8,128)(2,1)S(1)} %reshape.246, bf16[1,4,1024,1024]{2,3,1,0:T(8,128)(2,1)S(1)} %fusion.2), kind=kOutput, calls=%fused_computation.37 | convolution fusion | flops 1073741824 | bytes 9961472 | tf_op jit(solution)/shard_map/kgrc,rkgd->ckd/dot_general | solution.py:62
  120.7 3.6 %fusion.67 = f32[1024,1024,4]{1,0,2:T(8,128)S(1)} fusion(bf16[1024,128,1]{1,0,2:T(8,128)(2,1)S(1)} %bitcast.215, bf16[1024,4,128]{0,2,1:T(8,128)(2,1)} %copy-done.2), kind=kOutput, calls=%fused_computation.63 | convolution fusion | flops 1073741824 | bytes 18087936 | tf_op jit(solution)/shard_map/rkgd,ckd->kgrc/dot_general | solution.py:43
  124.2 9.7 %fusion.7 = bf16[1,4,1024,1024]{2,3,1,0:T(8,128)(2,1)} fusion(f32[1024,1024,4]{1,0,2:T(8,128)S(1)} %fusion.67, bf16[1024,128,1]{1,0,2:T(8,128)(2,1)} %bitcast.16, bf16[1024,4,128]{0,2,1:T(8,128)(2,1)} %copy-done.4, f32[4,1024]{1,0:T(4,128)S(1)} %bitcast.218, f32[4,1024]{1,0:T(4,128)S(1)} %bitcast.221, pred[1024,1024]{0,1:T(8,128)(4,1)} %get-tuple-element.10), kind=kOutput, calls=%fused_computation.10 | convolution fusion | flops 1103101952 | bytes 27557888 | tf_op jit(solution)/shard_map/rkgd,ckd->kgrc/dot_general | solution.py:55
  133.9 7.1 %fusion.20 = f32[4,1024,128]{2,1,0:T(8,128)} fusion(bf16[1024,128,1]{1,0,2:T(8,128)(2,1)S(1)} %bitcast.216, bf16[1,4,1024,1024]{2,3,1,0:T(8,128)(2,1)} %fusion.7), kind=kOutput, calls=%fused_computation.24 | convolution fusion | flops 1073741824 | bytes 10747904 | tf_op jit(solution)/shard_map/kgrc,ckd->rkgd/dot_general | solution.py:65
  141.0 6.1 %fusion.54 = bf16[1024,128]{1,0:T(8,128)(2,1)} fusion(f32[1024,128]{1,0:T(8,128)} %collective-permute-done.3, bf16[1024,4,128]{0,2,1:T(8,128)(2,1)} %copy-done.4, f32[1024,1024,4]{1,0,2:T(8,128)S(1)} %fusion.67, f32[4,1024]{1,0:T(4,128)S(1)} %bitcast.222, pred[1024,1024]{0,1:T(8,128)(4,1)} %get-tuple-element.10), kind=kOutput, calls=%fused_computation.43 | convolution fusion | flops 1090781184 | bytes 19677184 | tf_op jit(solution)/shard_map/kgrc,rkgd->ckd/dot_general | solution.py:59
  147.2 3.7 %all-to-all-start.8 = ((bf16[8,128,128]{2,1,0:T(8,128)(2,1)}), bf16[8,128,128]{2,1,0:T(8,128)(2,1)S(1)}, u32[]{:S(2)}, u32[]{:S(2)}) async-start(bf16[8,128,128]{2,1,0:T(8,128)(2,1)} %bitcast.51), calls=%async_computation.8 | async-start | bytes 524288 | tf_op jit(solution)/shard_map/all_to_all | solution.py:116
  150.9 6.8 %fusion.51 = bf16[1024,128]{1,0:T(8,128)(2,1)} fusion(f32[1024,128]{1,0:T(8,128)} %collective-permute-done.2, bf16[1024,4,128]{0,2,1:T(8,128)(2,1)} %copy-done.2, bf16[1,4,1024,1024]{2,3,1,0:T(8,128)(2,1)} %fusion.7), kind=kOutput, calls=%fused_computation.42 | convolution fusion | flops 1074003968 | bytes 10223616 | tf_op jit(solution)/shard_map/kgrc,rkgd->ckd/dot_general | solution.py:62
  158.2 4.9 %all-to-all-start.7 = ((bf16[8,128,128]{2,1,0:T(8,128)(2,1)}), bf16[8,128,128]{2,1,0:T(8,128)(2,1)S(1)}, u32[]{:S(2)}, u32[]{:S(2)}) async-start(bf16[8,128,128]{2,1,0:T(8,128)(2,1)} %bitcast.45), calls=%async_computation.7 | async-start | bytes 524288 | tf_op jit(solution)/shard_map/all_to_all | solution.py:115
  163.1 6.5 %fusion.30 = bf16[1024,1,4,128]{3,0,2,1:T(8,128)(2,1)S(1)} fusion(f32[4,1024,128]{2,1,0:T(8,128)} %fusion.20, bf16[1,4,1024,1024]{2,3,1,0:T(8,128)(2,1)} %copy-done.3, bf16[1024,128]{1,0:T(8,128)(2,1)} %collective-permute-done), kind=kOutput, calls=%fused_computation.35 | convolution fusion | flops 1074790400 | bytes 11796480 | tf_op jit(solution)/shard_map/kgrc,ckd->rkgd/dot_general | solution.py:65
  171.6 5.7 %all-to-all-start.6 = ((bf16[8,128,512]{1,2,0:T(8,128)(2,1)}), bf16[8,128,512]{1,2,0:T(8,128)(2,1)S(1)}, u32[]{:S(2)}, u32[]{:S(2)}) async-start(bf16[8,128,512]{1,2,0:T(8,128)(2,1)} %copy.69), calls=%async_computation.6 | async-start | bytes 2097152 | tf_op jit(solution)/shard_map/all_to_all | solution.py:114
  178.8 14.0 %all-to-all-done.6 = bf16[8,128,512]{1,2,0:T(8,128)(2,1)S(1)} async-done(((bf16[8,128,512]{1,2,0:T(8,128)(2,1)}), bf16[8,128,512]{1,2,0:T(8,128)(2,1)S(1)}, u32[]{:S(2)}, u32[]{:S(2)}) %all-to-all-start.6) | async-done | bytes 1048608 | tf_op jit(solution)/shard_map/all_to_all | solution.py:114
  (40 shorter events, 13.6 us)
Async XLA Ops:
  0.6 1.0 copy-start
  2.3 12.7 %all-to-all-start = ((bf16[128,8,128]{2,0,1:T(8,128)(2,1)}), bf16[128,8,128]{2,0,1:T(8,128)(2,1)S(1)}, u32[]{:S(2)}, u32[]{:S(2)}) async-start(bf16[128,8,128]{2,0,1:T(8,128)(2,1)} %copy_bitcast_fusion.3), calls=%async_computation | async-start | bytes 524288 | tf_op jit(solution)/shard_map/all_to_all | solution.py:86
  15.1 11.0 %all-to-all-start.3 = ((bf16[128,8,128]{2,0,1:T(8,128)(2,1)}), bf16[128,8,128]{2,0,1:T(8,128)(2,1)}, u32[]{:S(2)}, u32[]{:S(2)}) async-start(bf16[128,8,128]{2,0,1:T(8,128)(2,1)} %copy_bitcast_fusion.2), calls=%async_computation.3 | async-start | bytes 524288 | tf_op jit(solution)/shard_map/all_to_all | solution.py:87
  26.1 16.8 %all-to-all-start.1 = ((bf16[128,8,512]{0,2,1:T(8,128)(2,1)}), bf16[128,8,512]{0,2,1:T(8,128)(2,1)S(1)}, u32[]{:S(2)}, u32[]{:S(2)}) async-start(bf16[128,8,512]{0,2,1:T(8,128)(2,1)} %bitcast.5), calls=%async_computation.1 | async-start | bytes 2097152 | tf_op jit(solution)/shard_map/all_to_all | solution.py:85
  42.8 18.4 %all-to-all-start.4 = ((bf16[128,8,512]{0,2,1:T(8,128)(2,1)}), bf16[128,8,512]{0,2,1:T(8,128)(2,1)S(1)}, u32[]{:S(2)}, u32[]{:S(2)}) async-start(bf16[128,8,512]{0,2,1:T(8,128)(2,1)} %bitcast.17), calls=%async_computation.4 | async-start | bytes 2097152 | tf_op jit(solution)/shard_map/all_to_all | solution.py:89
  52.6 16.0 %collective-permute-start = (bf16[1024,128]{1,0:T(8,128)(2,1)S(1)}, bf16[1024,128]{1,0:T(8,128)(2,1)}, u32[]{:S(2)}, u32[]{:S(2)}) collective-permute-start(bf16[1024,128]{1,0:T(8,128)(2,1)S(1)} %bitcast.214), channel_id=1, source_target_pairs={{0,8},{8,16},{16,24},{24,32},{32,40},{40,48},{48,56},{56,64},{64,7... | collective-permute-start | bytes 786440 | tf_op jit(solution)/shard_map/ppermute | solution.py:13
  55.0 50.0 %collective-permute-start.1 = (bf16[1024,128]{1,0:T(8,128)(2,1)}, bf16[1024,128]{1,0:T(8,128)(2,1)}, u32[]{:S(2)}, u32[]{:S(2)}) collective-permute-start(bf16[1024,128]{1,0:T(8,128)(2,1)} %bitcast.15), channel_id=1, source_target_pairs={{0,8},{8,16},{16,24},{24,32},{32,40},{40,48},{48,56},{56,64},{64,7... | collective-permute-start | bytes 786440 | tf_op jit(solution)/shard_map/ppermute | solution.py:13
  57.7 59.5 %copy-start.2 = (bf16[1024,4,128]{0,2,1:T(8,128)(2,1)}, bf16[1024,4,128]{0,2,1:T(8,128)(2,1)S(1)}, u32[]{:S(2)}) copy-start(bf16[1024,4,128]{0,2,1:T(8,128)(2,1)S(1)} %reshape.246) | copy-start | bytes 3145732
  61.2 17.7 %all-to-all-start.2 = ((f32[128,8,4]{0,2,1:T(4,128)}), f32[128,8,4]{0,2,1:T(4,128)S(1)}, u32[]{:S(2)}, u32[]{:S(2)}) async-start(f32[128,8,4]{0,2,1:T(4,128)} %bitcast.9), calls=%async_computation.2 | async-start | bytes 32768 | tf_op jit(solution)/shard_map/all_to_all | solution.py:91
  78.8 14.2 %copy-start.4 = (bf16[1024,4,128]{0,2,1:T(8,128)(2,1)}, bf16[1024,4,128]{0,2,1:T(8,128)(2,1)S(1)}, u32[]{:S(2)}) copy-start(bf16[1024,4,128]{0,2,1:T(8,128)(2,1)S(1)} %reshape.249) | copy-start | bytes 3145732
  78.9 21.1 %all-to-all-start.5 = ((bf16[128,8,512]{0,2,1:T(8,128)(2,1)}), bf16[128,8,512]{0,2,1:T(8,128)(2,1)S(1)}, u32[]{:S(2)}, u32[]{:S(2)}) async-start(bf16[128,8,512]{0,2,1:T(8,128)(2,1)} %bitcast.210), calls=%async_computation.5 | async-start | bytes 2097152 | tf_op jit(solution)/shard_map/all_to_all | solution.py:88
  105.0 15.7 %copy-start.5 = (f32[1024,128]{1,0:T(8,128)S(1)}, f32[1024,128]{1,0:T(8,128)}, u32[]{:S(2)}) copy-start(f32[1024,128]{1,0:T(8,128)} %fusion.39) | copy-start | bytes 1572868
  117.2 3.5 %copy-start.3 = (bf16[1,4,1024,1024]{2,3,1,0:T(8,128)(2,1)}, bf16[1,4,1024,1024]{2,3,1,0:T(8,128)(2,1)S(1)}, u32[]{:S(2)}) copy-start(bf16[1,4,1024,1024]{2,3,1,0:T(8,128)(2,1)S(1)} %fusion.2) | copy-start | bytes 25165828
  120.7 30.2 %collective-permute-start.2 = (f32[1024,128]{1,0:T(8,128)}, f32[1024,128]{1,0:T(8,128)}, u32[]{:S(2)}, u32[]{:S(2)}) collective-permute-start(f32[1024,128]{1,0:T(8,128)} %fusion.36), channel_id=1, source_target_pairs={{0,120},{8,0},{16,8},{24,16},{32,24},{40,32},{48,40},{56,48},{64,5... | collective-permute-start | bytes 1572872 | tf_op jit(solution)/shard_map/ppermute | solution.py:13
  120.7 20.4 %collective-permute-start.3 = (f32[1024,128]{1,0:T(8,128)S(1)}, f32[1024,128]{1,0:T(8,128)}, u32[]{:S(2)}, u32[]{:S(2)}) collective-permute-start(f32[1024,128]{1,0:T(8,128)S(1)} %copy-done.5), channel_id=1, source_target_pairs={{0,120},{8,0},{16,8},{24,16},{32,24},{40,32},{48,40},{56,48},{64,5... | collective-permute-start | bytes 1572872 | tf_op jit(solution)/shard_map/ppermute | solution.py:13
  147.2 11.0 %all-to-all-start.8 = ((bf16[8,128,128]{2,1,0:T(8,128)(2,1)}), bf16[8,128,128]{2,1,0:T(8,128)(2,1)S(1)}, u32[]{:S(2)}, u32[]{:S(2)}) async-start(bf16[8,128,128]{2,1,0:T(8,128)(2,1)} %bitcast.51), calls=%async_computation.8 | async-start | bytes 524288 | tf_op jit(solution)/shard_map/all_to_all | solution.py:116
  150.9 43.2 %copy-start.1 = (bf16[128,1024]{1,0:T(8,128)(2,1)S(1)}, bf16[128,1024]{1,0:T(8,128)(2,1)}, u32[]{:S(2)}) copy-start(bf16[128,1024]{1,0:T(8,128)(2,1)} %param.8) | copy-start | bytes 786436
  158.2 13.4 %all-to-all-start.7 = ((bf16[8,128,128]{2,1,0:T(8,128)(2,1)}), bf16[8,128,128]{2,1,0:T(8,128)(2,1)S(1)}, u32[]{:S(2)}, u32[]{:S(2)}) async-start(bf16[8,128,128]{2,1,0:T(8,128)(2,1)} %bitcast.45), calls=%async_computation.7 | async-start | bytes 524288 | tf_op jit(solution)/shard_map/all_to_all | solution.py:115
  171.6 21.2 %all-to-all-start.6 = ((bf16[8,128,512]{1,2,0:T(8,128)(2,1)}), bf16[8,128,512]{1,2,0:T(8,128)(2,1)S(1)}, u32[]{:S(2)}, u32[]{:S(2)}) async-start(bf16[8,128,512]{1,2,0:T(8,128)(2,1)} %copy.69), calls=%async_computation.6 | async-start | bytes 2097152 | tf_op jit(solution)/shard_map/all_to_all | solution.py:114
where the time goes:
time: 195 us; the launch traced here: 194 us
  matrix products  72.9 us (37%)
  waiting for transfers between devices  46 us (24%)
  starting transfers between devices  45.8 us (23%)
  local copies, waits for them, and re-layouts  21.4 us (11%)
  other arithmetic  4.61 us (2%)
  between operations  3.39 us (2%)
    dot_general x2, matrix products, tile_grads(): jnp.einsum('rkgd,ckd->kgrc', gradient_per_head, value_per_head, preferred...  21.8 us
    dot_general x2, matrix products, tile_grads(): jnp.einsum('kgrc,rkgd->ckd', probs_low, gradient_per_head, preferred_elem...  14.6 us
    all_to_all x1, waiting for transfers between devices, body(): lax.all_to_all(grad_queries, 'uly', split_axis=0, concat_axis=1, tiled=True)  14 us
    dot_general x2, matrix products, tile_grads(): jnp.einsum('kgrc,ckd->rkgd', d_scores, key_per_head, preferred_element_ty...  13.7 us
    dot_general x2, matrix products, tile_grads(): jnp.einsum('rkgd,ckd->kgrc', query_per_head, key_per_head, preferred_elem...  12.6 us
    all_to_all x1, waiting for transfers between devices, body(): lax.all_to_all(queries, 'uly', split_axis=1, concat_axis=0, tiled=True)  10.9 us
    dot_general x2, matrix products, tile_grads(): jnp.einsum('kgrc,rkgd->ckd', d_scores, query_per_head, preferred_element_...  10.3 us
    unnamed x17, local copies, waits for them, and re-layouts  9.39 us
  transfers between devices with their start and end apart: 13, of which 7 were waited for; matrix products, arithmetic and copies ran while one was open for 41% of the time, Pallas kernels for 0%

commit v1 on v0

v1 whole, which is shorter than its diff:
```python
import functools
import math

import jax
import jax.numpy as jnp
from jax import lax
from jax.experimental import pallas as pl
from jax.experimental.pallas import tpu as pltpu
from jax.sharding import PartitionSpec as P

D = 128
N_ULY = 8
TOK = 128
GROUP = 4
HALF = 512
FACTOR = 1.0 / math.sqrt(D)
LOG2E = math.log2(math.e)
STAT = 32
BF = jnp.bfloat16
F32 = jnp.float32
MIB = 1 << 20


def nt(a, b):
    return lax.dot_general(a, b, (((1,), (1,)), ((), ())), preferred_element_type=F32)


def nn(a, b):
    return jnp.dot(a, b, preferred_element_type=F32)


def tn(a, b):
    return lax.dot_general(a, b, (((0,), (0,)), ((), ())), preferred_element_type=F32)


def pack_kernel(first, heads, with_kv, *refs):
    if with_kv:
        q_ref, do_ref, o_ref, lse_ref, k_ref, v_ref, msg_ref = refs
    else:
        q_ref, do_ref, o_ref, lse_ref, msg_ref = refs
    u = pl.program_id(0)
    lse_rows = jnp.transpose(lse_ref[...]) * LOG2E
    head_of = lax.broadcasted_iota(jnp.int32, lse_rows.shape, 0)
    row_of = lax.broadcasted_iota(jnp.int32, (8, D), 0)
    stats = jnp.zeros((8, TOK), F32)
    for j in range(heads):
        cols = slice(j * D, (j + 1) * D)
        msg_ref[0, j * TOK : (j + 1) * TOK, :] = q_ref[:, cols]
        msg_ref[0, (heads + j) * TOK : (heads + j + 1) * TOK, :] = do_ref[:, cols]
        product = do_ref[:, cols].astype(F32) * o_ref[:, cols].astype(F32)
        high = product.astype(BF)
        low = (product - high.astype(F32)).astype(BF)
        ones = jnp.where(row_of == heads + j, 1.0, 0.0).astype(BF)
        stats = stats + nt(ones, high) + nt(ones, low)
        lse_one = jnp.sum(
            jnp.where(head_of == u * GROUP + first + j, lse_rows, 0.0), axis=0, keepdims=True
        )
        stats = stats + jnp.where(row_of == j, lse_one, 0.0)
    at = 2 * heads * TOK
    if with_kv:
        msg_ref[0, at : at + TOK, :] = k_ref[...]
        msg_ref[0, at + TOK : at + 2 * TOK, :] = v_ref[...]
        at += 2 * TOK
    p0 = stats.astype(BF).astype(F32)
    p1 = (stats - p0).astype(BF).astype(F32)
    p2 = stats - p0 - p1
    pieces = jnp.concatenate([p0, p1, p2, jnp.zeros_like(p0)], axis=0)
    msg_ref[0, at : at + STAT, :] = pieces.astype(BF)


def pack(queries, grads, outputs, lse, kv, first, heads):
    rows = 2 * heads * TOK + STAT + (2 * TOK if kv else 0)
    per = GROUP // heads
    wide = pl.BlockSpec((TOK, heads * D), lambda u: (0, per * u + first // heads))
    one = pl.BlockSpec((TOK, D), lambda u: (0, u))
    return pl.pallas_call(
        functools.partial(pack_kernel, first, heads, bool(kv)),
        grid=(N_ULY,),
        in_specs=[wide, wide, wide, pl.BlockSpec(lse.shape, lambda u: (0, 0))] + [one] * len(kv),
        out_specs=pl.BlockSpec((1, rows, D), lambda u: (u, 0, 0)),
        out_shape=jax.ShapeDtypeStruct((N_ULY, rows, D), BF),
        name="pack_heads_%d" % first,
        cost_estimate=pl.CostEstimate(flops=10 * MIB, bytes_accessed=4 * MIB, transcendentals=0),
    )(queries, grads, outputs, lse, *kv)


def slots_of(order_ref):
    slot = lax.axis_index("blk")
    prev = lax.rem(slot + 15, 16)
    a, b = order_ref[slot, 0], order_ref[slot, 1]
    pa, pb = order_ref[prev, 0], order_ref[prev, 1]
    low = (a > b).astype(jnp.int32)
    prev_low = (pa > pb).astype(jnp.int32)
    lower_sees = jnp.minimum(a, b) > jnp.minimum(pa, pb)
    return low, prev_low, lower_sees


def half(ref, which, at):
    return ref[pl.ds(which * 4, 4), at : at + TOK, :].reshape(HALF, D)


def tile(q, do, lse, delta, k, v, shift):
    scores = nt(k, q)
    probs = jnp.exp2(scores * (FACTOR * LOG2E) - lse)
    if shift is not None:
        key = lax.broadcasted_iota(jnp.int32, probs.shape, 0)
        row = lax.broadcasted_iota(jnp.int32, probs.shape, 1)
        probs = jnp.where(row + shift >= key, probs, 0.0)
    d_probs = nt(v, do)
    d_scores = (probs * (d_probs - delta) * FACTOR).astype(BF)
    return nn(probs.astype(BF), do), nn(d_scores, q), tn(d_scores, k)


def stat_rows(x_ref, at):
    blocks = []
    for s in range(N_ULY):
        p = x_ref[s, at : at + STAT, :].astype(F32)
        blocks.append(p[0:8] + p[8:16] + p[16:24])
    return jnp.concatenate(blocks, axis=1)


def pick(stats, row, which):
    lower, upper = stats[row : row + 1, :HALF], stats[row : row + 1, HALF:]
    return jnp.where(which == 0, lower, upper)


def head_views(x_ref, stats, heads, j, which):
    return (
        half(x_ref, which, j * TOK),
        half(x_ref, which, (heads + j) * TOK),
        pick(stats, j, which),
        pick(stats, heads + j, which),
    )


def add_to(ref, index, which, value):
    ref[index, pl.ds(which * 4, 4)] += value.reshape(4, TOK, D)


def local_head(low, x_ref, stats, heads, j, k_ref, k_at, dq_ref, dkv_ref):
    high = 1 - low
    k_low, v_low = half(k_ref, low, k_at), half(k_ref, low, k_at + TOK)
    k_high, v_high = half(k_ref, high, k_at), half(k_ref, high, k_at + TOK)
    rows_low = head_views(x_ref, stats, heads, j, low)
    rows_high = head_views(x_ref, stats, heads, j, high)

    def diagonal(rows, k, v):
        q, do, lse, delta = rows
        dv0, dk0, dq0 = tile(q, do, lse, delta, k[:256], v[:256], 0)
        dv1, dk1, dq1 = tile(
            q[256:], do[256:], lse[:, 256:], delta[:, 256:], k[256:], v[256:], 0
        )
        dq = jnp.concatenate([dq0[:256], dq0[256:] + dq1], axis=0)
        return jnp.concatenate([dv0, dv1], 0), jnp.concatenate([dk0, dk1], 0), dq

    dv, dk, dq = tile(*rows_high, k_low, v_low, None)
    dv2, dk2, dq2 = diagonal(rows_high, k_high, v_high)
    add_to(dkv_ref, 0, high, dk2)
    add_to(dkv_ref, 1, high, dv2)
    dq_ref[pl.ds(high * 4, 4)] += (dq + dq2).reshape(4, TOK, D)
    dv3, dk3, dq3 = diagonal(rows_low, k_low, v_low)
    add_to(dkv_ref, 0, low, dk + dk3)
    add_to(dkv_ref, 1, low, dv + dv3)
    dq_ref[pl.ds(low * 4, 4)] += dq3.reshape(4, TOK, D)


def cross_head(low, prev_low, lower_sees, x_ref, stats, heads, j, kp_ref, dq_ref, dkv_ref):
    high = 1 - low
    k_low, v_low = half(kp_ref, prev_low, 0), half(kp_ref, prev_low, TOK)
    rows_high = head_views(x_ref, stats, heads, j, high)
    dv, dk, dq = tile(*rows_high, k_low, v_low, None)
    add_to(dkv_ref, 0, prev_low, dk)
    add_to(dkv_ref, 1, prev_low, dv)
    dq_ref[pl.ds(high * 4, 4)] += dq.reshape(4, TOK, D)
    sees = lower_sees.astype(jnp.int32)
    rows_at = sees * low + (1 - sees) * high
    keys_at = sees * prev_low + (1 - sees) * (1 - prev_low)
    k, v = half(kp_ref, keys_at, 0), half(kp_ref, keys_at, TOK)
    rows = head_views(x_ref, stats, heads, j, rows_at)
    dv, dk, dq = tile(*rows, k, v, None)
    add_to(dkv_ref, 0, keys_at, dk)
    add_to(dkv_ref, 1, keys_at, dv)
    dq_ref[pl.ds(rows_at * 4, 4)] += dq.reshape(4, TOK, D)


def first_kernel(heads, order_ref, x_ref, kp_ref, dq_out, local_out, cross_out, dq_acc):
    low, prev_low, lower_sees = slots_of(order_ref)
    kv_at = 2 * heads * TOK
    stats = stat_rows(x_ref, kv_at + 2 * TOK)
    local_out[...] = jnp.zeros_like(local_out)
    cross_out[...] = jnp.zeros_like(cross_out)
    for j in range(heads):
        dq_acc[...] = jnp.zeros_like(dq_acc)
        local_head(low, x_ref, stats, heads, j, x_ref, kv_at, dq_acc, local_out)
        cross_head(
            low, prev_low, lower_sees, x_ref, stats, heads, j, kp_ref, dq_acc, cross_out
        )
        dq_out[:, j * TOK : (j + 1) * TOK, :] = dq_acc[...].astype(BF)


def cross_kernel(heads, order_ref, x_ref, kp_ref, cross_in, dq_out, cross_out, acc):
    low, prev_low, lower_sees = slots_of(order_ref)
    stats = stat_rows(x_ref, 2 * heads * TOK)
    acc[...] = cross_in[...]
    dq_out[...] = jnp.zeros_like(dq_out)
    for j in range(heads):
        cross_head(
            low, prev_low, lower_sees, x_ref, stats, heads, j, kp_ref, dq_out.at[j], acc
        )
    cross_out[...] = acc[...].astype(BF)


def local_kernel(heads, kv_at, order_ref, x_ref, x0_ref, dq_in, local_in, dq_out, local_out, acc):
    low, _, _ = slots_of(order_ref)
    stats = stat_rows(x_ref, 2 * heads * TOK)
    local_out[...] = local_in[...]
    for j in range(heads):
        acc[...] = dq_in[j]
        local_head(low, x_ref, stats, heads, j, x0_ref, kv_at, acc, local_out)
        dq_out[:, j * TOK : (j + 1) * TOK, :] = acc[...].astype(BF)


def add_kernel(msg_in, local_ref, back_ref, msg_out):
    del msg_in
    total = local_ref[...] + back_ref[...].astype(F32)
    msg_out[:, 0:TOK, :] = total[0].astype(BF)
    msg_out[:, TOK : 2 * TOK, :] = total[1].astype(BF)


def unpack_kernel(heads, a_ref, b_ref, dq_ref, dk_ref, dv_ref):
    for j in range(heads):
        dq_ref[:, j * D : (j + 1) * D] = a_ref[0, j * TOK : (j + 1) * TOK, :]
        at = (heads + j) * D
        dq_ref[:, at : at + D] = b_ref[0, j * TOK : (j + 1) * TOK, :]
    dk_ref[...] = b_ref[0, heads * TOK : (heads + 1) * TOK, :]
    dv_ref[...] = b_ref[0, (heads + 1) * TOK : (heads + 2) * TOK, :]


def vmem():
    return pl.BlockSpec(memory_space=pltpu.VMEM)


def smem():
    return pl.BlockSpec(memory_space=pltpu.SMEM)


def params():
    return pltpu.CompilerParams(vmem_limit_bytes=40 * MIB)


def shift_slot(value, by):
    length = lax.axis_size("blk")
    return lax.ppermute(value, "blk", [(i, (i + by) % length) for i in range(length)])


def exchange(value):
    return lax.all_to_all(value, "uly", split_axis=0, concat_axis=0, tiled=True)


def body(queries, input_keys, input_values, outputs, output_gradient, saved_logsumexp, span_order):
    h = 2
    kv_at = 2 * h * TOK
    rows4 = (N_ULY, TOK, D)
    msg0 = pack(
        queries, output_gradient, outputs, saved_logsumexp, (input_keys, input_values), 0, h
    )
    x0 = exchange(msg0)
    msg1 = pack(queries, output_gradient, outputs, saved_logsumexp, (), h, h)
    x1 = exchange(msg1)
    kv_prev = shift_slot(x0[:, kv_at : kv_at + 2 * TOK, :], 1)

    def cost(units):
        return pl.CostEstimate(
            flops=units * h * 5 * 2 * 512 * 512 * 128 * 2,
            bytes_accessed=4 * MIB,
            transcendentals=units * h * 512 * 512,
        )

    dq0, local, cross = pl.pallas_call(
        functools.partial(first_kernel, h),
        in_specs=[smem(), vmem(), vmem()],
        out_specs=[vmem()] * 3,
        out_shape=[
            jax.ShapeDtypeStruct((N_ULY, h * TOK, D), BF),
            jax.ShapeDtypeStruct((2,) + rows4, F32),
            jax.ShapeDtypeStruct((2,) + rows4, F32),
        ],
        scratch_shapes=[pltpu.VMEM(rows4, F32)],
        compiler_params=params(),
        cost_estimate=cost(5),
        name="first_heads",
    )(span_order, x0, kv_prev)
    r0 = exchange(dq0)
    dq1, cross_low = pl.pallas_call(
        functools.partial(cross_kernel, h),
        in_specs=[smem(), vmem(), vmem(), vmem()],
        out_specs=[vmem()] * 2,
        out_shape=[
            jax.ShapeDtypeStruct((h,) + rows4, F32),
            jax.ShapeDtypeStruct((2,) + rows4, BF),
        ],
        scratch_shapes=[pltpu.VMEM((2,) + rows4, F32)],
        compiler_params=params(),
        cost_estimate=cost(2),
        name="cross_heads",
    )(span_order, x1, kv_prev, cross)
    back = shift_slot(cross_low, -1)
    dq1, local = pl.pallas_call(
        functools.partial(local_kernel, h, kv_at),
        in_specs=[smem()] + [vmem()] * 4,
        out_specs=[vmem()] * 2,
        out_shape=[
            jax.ShapeDtypeStruct((N_ULY, h * TOK, D), BF),
            jax.ShapeDtypeStruct((2,) + rows4, F32),
        ],
        scratch_shapes=[pltpu.VMEM(rows4, F32)],
        compiler_params=params(),
        cost_estimate=cost(3),
        name="local_heads",
    )(span_order, x1, x0, dq1, local)
    dkv = (local + back.astype(F32)).astype(BF)
    msg = jnp.concatenate([dq1, dkv[0], dkv[1]], axis=1)
    r1 = exchange(msg)
    return pl.pallas_call(
        functools.partial(unpack_kernel, h),
        grid=(N_ULY,),
        in_specs=[
            pl.BlockSpec((1, h * TOK, D), lambda u: (u, 0, 0)),
            pl.BlockSpec((1, (h + 2) * TOK, D), lambda u: (u, 0, 0)),
        ],
        out_specs=[
            pl.BlockSpec((TOK, GROUP * D), lambda u: (0, u)),
            pl.BlockSpec((TOK, D), lambda u: (0, u)),
            pl.BlockSpec((TOK, D), lambda u: (0, u)),
        ],
        out_shape=[
            jax.ShapeDtypeStruct((TOK, N_ULY * GROUP * D), BF),
            jax.ShapeDtypeStruct((TOK, N_ULY * D), BF),
            jax.ShapeDtypeStruct((TOK, N_ULY * D), BF),
        ],
        name="unpack",
    )(r0, r1)


def solution(mesh):
    rows = P(("blk", "uly"), None)
    return jax.shard_map(
        body, mesh=mesh, in_specs=(rows,) * 6 + (P(),), out_specs=(rows,) * 3, check_vma=False
    )
```

time: 195 us -> 115 us (0.59)
  the two profiles are of different devices: /device:TPU:64 before, /device:TPU:6 now
where the time goes in v1:
time: 115 us; the launch traced here: 114 us
  blocking collectives  47.5 us (41%)
  Pallas kernels  36.5 us (32%)
  starting transfers between devices  11.1 us (10%)
  local copies, waits for them, and re-layouts  8.99 us (8%)
  waiting for transfers between devices  7.75 us (7%)
  other arithmetic  1.24 us (1%)
    all_to_all x2, blocking collectives, exchange(): return lax.all_to_all(value, 'uly', split_axis=0, concat_axis=0, tiled=True)  47.5 us
    pallas_call x2, Pallas kernels, pack(): pl.pallas_call(functools.partial(pack_kernel, first, heads, bool(kv)), gr...  12.3 us
    pallas_call x1, Pallas kernels, body(): pl.pallas_call(functools.partial(first_kernel, h), in_specs=[smem(), vmem...  8.79 us
    unnamed x18, local copies, waits for them, and re-layouts  8.12 us
    all_to_all x2, waiting for transfers between devices, exchange(): return lax.all_to_all(value, 'uly', split_axis=0, concat_axis=0, tiled=True)  7.74 us
    all_to_all x2, starting transfers between devices, exchange(): return lax.all_to_all(value, 'uly', split_axis=0, concat_axis=0, tiled=True)  7.18 us
    pallas_call x1, Pallas kernels, body(): pl.pallas_call(functools.partial(unpack_kernel, h), grid=(N_ULY,), in_spe...  5.5 us
    pallas_call x1, Pallas kernels, body(): pl.pallas_call(functools.partial(local_kernel, h, kv_at), in_specs=[smem(...  5.23 us
  transfers between devices with their start and end apart: 4, of which 2 were waited for; matrix products, arithmetic and copies ran while one was open for 1% of the time, Pallas kernels for 18%

profile of v1, /device:TPU:6, one launch (start us, length us, event | category | flops | bytes accessed | tf_op | source)
XLA Modules:
  0.0 113.7 jit_solution(8640970455322570058)
XLA Ops:
  0.6 1.4 %copy.10.refs_3_ = f32[128,32]{1,0:T(8,128)} copy(f32[128,32]{0,1:T(8,128)} %param.12) | data formatting | bytes 32768 | tf_op args[5]
  2.1 6.3 %pack_heads_0.1 = bf16[8,800,128]{2,1,0:T(8,128)(2,1)} custom-call(bf16[128,4096]{1,0:T(8,128)(2,1)} %refs_0_.3, bf16[128,4096]{1,0:T(8,128)(2,1)} %refs_1_.3, bf16[128,4096]{1,0:T(8,128)(2,1)} %refs_2_.3, f32[128,32]{1,0:T(8,128)} %copy.10.refs_3_, bf16[128,1024]{1,0:T(8,128)(2,1)} %refs_4_.1, bf16[128,1024]{1,0:T(8,128)(2,1)} %refs_5_.1), custom_call_target="tpu_custom_call" | custom-call | flops 10485760 | bytes 4194304 | tf_op jit(solution)/shard_map/pack_heads_0/pallas_call | solution.py:76
  8.4 28.0 %all_to_all.20.x_ref.x0_ref = bf16[8,800,128]{2,1,0:T(8,128)(2,1)S(1)} all-to-all(bf16[8,800,128]{2,1,0:T(8,128)(2,1)} %pack_heads_0.1), channel_id=1, replica_groups=mesh['blk'=16,'uly'=8] {'uly'}, dimensions={0} | all-to-all | bytes 3276800 | tf_op jit(solution)/shard_map/all_to_all | solution.py:257
  36.4 0.8 slice.12
  37.2 0.0 collective-permute-start
  37.2 6.0 %pack_heads_2.1 = bf16[8,544,128]{2,1,0:T(8,128)(2,1)} custom-call(bf16[128,4096]{1,0:T(8,128)(2,1)} %refs_0_.3, bf16[128,4096]{1,0:T(8,128)(2,1)} %refs_1_.3, bf16[128,4096]{1,0:T(8,128)(2,1)} %refs_2_.3, f32[128,32]{1,0:T(8,128)} %copy.10.refs_3_), custom_call_target="tpu_custom_call" | custom-call | flops 10485760 | bytes 4194304 | tf_op jit(solution)/shard_map/pack_heads_2/pallas_call | solution.py:76
  43.2 0.0 copy-start.7
  43.2 3.7 %all-to-all-start.2 = ((bf16[8,544,128]{2,1,0:T(8,128)(2,1)}), bf16[8,544,128]{2,1,0:T(8,128)(2,1)S(1)}, u32[]{:S(2)}, u32[]{:S(2)}) async-start(bf16[8,544,128]{2,1,0:T(8,128)(2,1)} %pack_heads_2.1), calls=%async_computation.2 | async-start | bytes 2228224 | tf_op jit(solution)/shard_map/all_to_all | solution.py:257
  46.9 0.0 copy-done.7
  46.9 0.1 copy.11.order_ref
  47.0 0.0 collective-permute-done.kp_ref
  47.0 8.8 %first_heads.1 = (bf16[8,256,128]{2,1,0:T(8,128)(2,1)}, f32[2,8,128,128]{3,2,1,0:T(8,128)S(1)}, f32[2,8,128,128]{3,2,1,0:T(8,128)S(1)}) custom-call(s32[16,2]{1,0:T(8,128)S(1)} %copy.11.order_ref, bf16[8,800,128]{2,1,0:T(8,128)(2,1)S(1)} %all_to_all.20.x_ref.x0_ref, bf16[8,256,128]{2,1,0:T(8,128)(2,1)S(1)} %collective-permute-done.kp_ref), custom_call_target="tpu_custom_call" | custom-call | flops 6710886400 | bytes 4194304 | tf_op jit(solution)/shard_map/first_heads/pallas_call | solution.py:279
  55.8 0.0 copy-start.2
  55.8 1.0 copy-done.2
  56.8 1.0 copy-done.4
  57.7 4.8 %all-to-all-done.2.x_ref = bf16[8,544,128]{2,1,0:T(8,128)(2,1)S(1)} async-done(((bf16[8,544,128]{2,1,0:T(8,128)(2,1)}), bf16[8,544,128]{2,1,0:T(8,128)(2,1)S(1)}, u32[]{:S(2)}, u32[]{:S(2)}) %all-to-all-start.2) | async-done | bytes 1114144 | tf_op jit(solution)/shard_map/all_to_all | solution.py:257
  62.5 1.2 %copy-done.3 = f32[2,8,128,128]{3,2,1,0:T(8,128)S(1)} copy-done((f32[2,8,128,128]{3,2,1,0:T(8,128)S(1)}, f32[2,8,128,128]{3,2,1,0:T(8,128)}, u32[]{:S(2)}) %copy-start.3) | copy-done | bytes 1048600
  63.7 4.7 %cross_heads.1 = (f32[2,8,128,128]{3,2,1,0:T(8,128)S(1)}, bf16[2,8,128,128]{3,2,1,0:T(8,128)(2,1)}) custom-call(s32[16,2]{1,0:T(8,128)S(1)} %copy.11.order_ref, bf16[8,544,128]{2,1,0:T(8,128)(2,1)S(1)} %all-to-all-done.2.x_ref, bf16[8,256,128]{2,1,0:T(8,128)(2,1)S(1)} %collective-permute-done.kp_ref, f32[2,8,128,128]{3,2,1,0:T(8,128)S(1)} %copy-done.3), custom_call_target="tpu_custom_call" | custom-call | flops 2684354560 | bytes 4194304 | tf_op jit(solution)/shard_map/cross_heads/pallas_call | solution.py:294
  68.5 1.0 copy-done
  69.4 3.9 %collective-permute-start.1 = (bf16[2,8,128,128]{3,2,1,0:T(8,128)(2,1)}, bf16[2,8,128,128]{3,2,1,0:T(8,128)(2,1)}, u32[]{:S(2)}, u32[]{:S(2)}) collective-permute-start(bf16[2,8,128,128]{3,2,1,0:T(8,128)(2,1)} %get-tuple-element.16), channel_id=1, source_target_pairs={{0,120},{8,0},{16,8},{24,16},{32,24},{40,32},{48,40},{56,48},{64,5... | collective-permute-start | bytes 1572872 | tf_op jit(solution)/shard_map/ppermute | solution.py:253
  73.3 3.5 %all-to-all-start.1 = ((bf16[8,256,128]{2,1,0:T(8,128)(2,1)}), bf16[8,256,128]{2,1,0:T(8,128)(2,1)S(1)}, u32[]{:S(2)}, u32[]{:S(2)}) async-start(bf16[8,256,128]{2,1,0:T(8,128)(2,1)} %get-tuple-element.10), calls=%async_computation.1 | async-start | bytes 1048576 | tf_op jit(solution)/shard_map/all_to_all | solution.py:257
  76.8 0.0 copy-start.1
  76.8 1.2 %copy-done.1 = f32[2,8,128,128]{3,2,1,0:T(8,128)S(1)} copy-done((f32[2,8,128,128]{3,2,1,0:T(8,128)S(1)}, f32[2,8,128,128]{3,2,1,0:T(8,128)}, u32[]{:S(2)}) %copy-start.1) | copy-done | bytes 1048600
  78.1 1.2 %copy-done.5 = f32[2,8,128,128]{3,2,1,0:T(8,128)S(1)} copy-done((f32[2,8,128,128]{3,2,1,0:T(8,128)S(1)}, f32[2,8,128,128]{3,2,1,0:T(8,128)}, u32[]{:S(2)}) %copy-start.5) | copy-done | bytes 1048600
  79.3 5.2 %local_heads.1 = (bf16[8,256,128]{2,1,0:T(8,128)(2,1)S(1)}, f32[2,8,128,128]{3,2,1,0:T(8,128)S(1)}) custom-call(s32[16,2]{1,0:T(8,128)S(1)} %copy.11.order_ref, bf16[8,544,128]{2,1,0:T(8,128)(2,1)S(1)} %all-to-all-done.2.x_ref, bf16[8,800,128]{2,1,0:T(8,128)(2,1)S(1)} %all_to_all.20.x_ref.x0_ref, f32[2,8,128,128]{3,2,1,0:T(8,128)S(1)} %copy-done.1, ...), custom_call_target="tpu_custom_call" | custom-call | flops 4026531840 | bytes 4194304 | tf_op jit(solution)/shard_map/local_heads/pallas_call | solution.py:308
  84.5 0.0 collective-permute-done.1
  84.5 1.2 %add_convert_fusion = bf16[2,8,128,128]{3,2,1,0:T(8,128)(2,1)S(1)} fusion(f32[2,8,128,128]{3,2,1,0:T(8,128)S(1)} %get-tuple-element.15, bf16[2,8,128,128]{3,2,1,0:T(8,128)(2,1)} %collective-permute-done.1), kind=kLoop, calls=%fused_computation.1 | loop fusion | flops 786432 | bytes 2097152 | tf_op jit(solution)/shard_map/convert_element_type | solution.py:321
  85.7 0.1 pad_maximum_fusion
  85.8 3.0 %all-to-all-done.1.a_ref = bf16[8,256,128]{2,1,0:T(8,128)(2,1)S(1)} async-done(((bf16[8,256,128]{2,1,0:T(8,128)(2,1)}), bf16[8,256,128]{2,1,0:T(8,128)(2,1)S(1)}, u32[]{:S(2)}, u32[]{:S(2)}) %all-to-all-start.1) | async-done | bytes 524320 | tf_op jit(solution)/shard_map/all_to_all | solution.py:257
  88.8 19.4 %all_to_all.21.b_ref = bf16[8,512,128]{2,1,0:T(8,128)(2,1)} all-to-all(bf16[8,512,128]{2,1,0:T(8,128)(2,1)S(1)} %pad_maximum_fusion), channel_id=1, replica_groups=mesh['blk'=16,'uly'=8] {'uly'}, dimensions={0} | all-to-all | bytes 2097152 | tf_op jit(solution)/shard_map/all_to_all | solution.py:257
  108.2 0.0 copy-done.6
  108.2 5.5 %unpack.1 = (bf16[128,4096]{1,0:T(8,128)(2,1)}, bf16[128,1024]{1,0:T(8,128)(2,1)}, bf16[128,1024]{1,0:T(8,128)(2,1)}) custom-call(bf16[8,256,128]{2,1,0:T(8,128)(2,1)} %copy-done.6, bf16[8,512,128]{2,1,0:T(8,128)(2,1)} %all_to_all.21.b_ref), custom_call_target="tpu_custom_call" | custom-call | tf_op jit(solution)/shard_map/unpack/pallas_call | solution.py:324
  (6 shorter events, 0.1 us)
Async XLA Ops:
  37.2 9.8 %collective-permute-start = (bf16[8,256,128]{2,1,0:T(8,128)(2,1)}, bf16[8,256,128]{2,1,0:T(8,128)(2,1)S(1)}, u32[]{:S(2)}, u32[]{:S(2)}) collective-permute-start(bf16[8,256,128]{2,1,0:T(8,128)(2,1)} %slice.12), channel_id=1, source_target_pairs={{0,8},{8,16},{16,24},{24,32},{32,40},{40,48},{48,56},{56,64},{64,7... | collective-permute-start | bytes 1572872 | tf_op jit(solution)/shard_map/ppermute | solution.py:253
  43.2 3.7 %copy-start.7 = (s32[16,2]{0,1:T(2,128)S(1)}, s32[16,2]{0,1:T(2,128)}, u32[]{:S(2)}) copy-start(s32[16,2]{0,1:T(2,128)} %param.13) | copy-start | bytes 388
  43.2 19.3 %all-to-all-start.2 = ((bf16[8,544,128]{2,1,0:T(8,128)(2,1)}), bf16[8,544,128]{2,1,0:T(8,128)(2,1)S(1)}, u32[]{:S(2)}, u32[]{:S(2)}) async-start(bf16[8,544,128]{2,1,0:T(8,128)(2,1)} %pack_heads_2.1), calls=%async_computation.2 | async-start | bytes 2228224 | tf_op jit(solution)/shard_map/all_to_all | solution.py:257
  55.8 1.0 copy-start.2
  56.8 1.0 copy-start.4
  62.5 1.2 %copy-start.3 = (f32[2,8,128,128]{3,2,1,0:T(8,128)S(1)}, f32[2,8,128,128]{3,2,1,0:T(8,128)}, u32[]{:S(2)}) copy-start(f32[2,8,128,128]{3,2,1,0:T(8,128)} %copy-done.2) | copy-start | bytes 3145732
  68.5 1.0 copy-start
  69.4 15.1 %collective-permute-start.1 = (bf16[2,8,128,128]{3,2,1,0:T(8,128)(2,1)}, bf16[2,8,128,128]{3,2,1,0:T(8,128)(2,1)}, u32[]{:S(2)}, u32[]{:S(2)}) collective-permute-start(bf16[2,8,128,128]{3,2,1,0:T(8,128)(2,1)} %get-tuple-element.16), channel_id=1, source_target_pairs={{0,120},{8,0},{16,8},{24,16},{32,24},{40,32},{48,40},{56,48},{64,5... | collective-permute-start | bytes 1572872 | tf_op jit(solution)/shard_map/ppermute | solution.py:253
  73.3 15.5 %all-to-all-start.1 = ((bf16[8,256,128]{2,1,0:T(8,128)(2,1)}), bf16[8,256,128]{2,1,0:T(8,128)(2,1)S(1)}, u32[]{:S(2)}, u32[]{:S(2)}) async-start(bf16[8,256,128]{2,1,0:T(8,128)(2,1)} %get-tuple-element.10), calls=%async_computation.1 | async-start | bytes 1048576 | tf_op jit(solution)/shard_map/all_to_all | solution.py:257
  76.8 1.2 %copy-start.1 = (f32[2,8,128,128]{3,2,1,0:T(8,128)S(1)}, f32[2,8,128,128]{3,2,1,0:T(8,128)}, u32[]{:S(2)}) copy-start(f32[2,8,128,128]{3,2,1,0:T(8,128)} %copy-done) | copy-start | bytes 3145732
  78.1 1.2 %copy-start.5 = (f32[2,8,128,128]{3,2,1,0:T(8,128)S(1)}, f32[2,8,128,128]{3,2,1,0:T(8,128)}, u32[]{:S(2)}) copy-start(f32[2,8,128,128]{3,2,1,0:T(8,128)} %copy-done.4) | copy-start | bytes 3145732
  88.8 19.4 %copy-start.6 = (bf16[8,256,128]{2,1,0:T(8,128)(2,1)}, bf16[8,256,128]{2,1,0:T(8,128)(2,1)S(1)}, u32[]{:S(2)}) copy-start(bf16[8,256,128]{2,1,0:T(8,128)(2,1)S(1)} %all-to-all-done.1.a_ref) | copy-start | bytes 1572868

commit v2 on v0

v2 whole, which is shorter than its diff:
```python
import functools
import math

import jax
import jax.numpy as jnp
from jax import lax
from jax.experimental import pallas as pl
from jax.experimental.pallas import tpu as pltpu
from jax.sharding import PartitionSpec as P

D = 128
N_ULY = 8
TOK = 128
GROUP = 4
HALF = 512
FACTOR = 1.0 / math.sqrt(D)
LOG2E = math.log2(math.e)
STAT = 32
BF = jnp.bfloat16
F32 = jnp.float32
MIB = 1 << 20


def nt(a, b):
    return lax.dot_general(a, b, (((1,), (1,)), ((), ())), preferred_element_type=F32)


def nn(a, b):
    return jnp.dot(a, b, preferred_element_type=F32)


def tn(a, b):
    return lax.dot_general(a, b, (((0,), (0,)), ((), ())), preferred_element_type=F32)


def copy_of(source, target, sem):
    return pltpu.make_async_copy(source, target, sem)


def head_group(u):
    upper = lax.axis_index("blk") // 8
    return u + upper * (1 - 2 * (u % 2))


def pack_kernel(first, heads, with_kv, *refs):
    if with_kv:
        q_ref, do_ref, o_ref, lse_hbm, k_ref, v_ref, msg_ref, buf, o_buf, lse_ref, sem = refs
    else:
        q_ref, do_ref, o_ref, lse_hbm, msg_ref, buf, o_buf, lse_ref, sem = refs
    rows = 2 * heads * TOK + (2 * TOK if with_kv else 0)
    lse_load = copy_of(lse_hbm, lse_ref, sem.at[3, 0])
    lse_load.start()

    for u in range(N_ULY):
        group = head_group(u)

        def load(source, column, at):
            cols = pl.ds(pl.multiple_of(column * D, D), D)
            copy_of(source.at[:, cols], buf.at[u, pl.ds(at, TOK), :], sem.at[0, u]).start()

        o_cols = pl.ds(pl.multiple_of((group * GROUP + first) * D, D), heads * D)
        copy_of(o_ref.at[:, o_cols], o_buf.at[u], sem.at[1, u]).start()
        for j in range(heads):
            load(do_ref, group * GROUP + first + j, (heads + j) * TOK)
        for j in range(heads):
            load(q_ref, group * GROUP + first + j, j * TOK)
        if with_kv:
            load(k_ref, group, 2 * heads * TOK)
            load(v_ref, group, (2 * heads + 1) * TOK)
    row_of = lax.broadcasted_iota(jnp.int32, (8, D), 0)
    lse_load.wait()
    for u in range(N_ULY):
        loaded = buf.at[u, pl.ds(0, rows), :]
        copy_of(loaded, loaded, sem.at[0, u]).wait()
        copy_of(o_buf.at[u], o_buf.at[u], sem.at[1, u]).wait()
        at = head_group(u) * GROUP + first
        stats = jnp.zeros((8, TOK), F32)
        for j in range(heads):
            grads = buf[u, (heads + j) * TOK : (heads + j + 1) * TOK, :].astype(F32)
            product = grads * o_buf[u, :, j * D : (j + 1) * D].astype(F32)
            high = product.astype(BF)
            low = (product - high.astype(F32)).astype(BF)
            ones = jnp.where(row_of == heads + j, 1.0, 0.0).astype(BF)
            stats = stats + nt(ones, high) + nt(ones, low)
            lse_one = lse_ref[pl.ds(at + j, 1), :] * LOG2E
            stats = stats + jnp.where(row_of == j, lse_one, 0.0)
        p0 = stats.astype(BF).astype(F32)
        p1 = (stats - p0).astype(BF).astype(F32)
        p2 = stats - p0 - p1
        pieces = jnp.concatenate([p0, p1, p2, jnp.zeros_like(p0)], axis=0)
        buf[u, rows : rows + STAT, :] = pieces.astype(BF)
        copy_of(buf.at[u], msg_ref.at[u], sem.at[2, u]).start()
    for u in range(N_ULY):
        copy_of(buf.at[u], msg_ref.at[u], sem.at[2, u]).wait()


def pack(queries, grads, outputs, lse, kv, first, heads):
    rows = 2 * heads * TOK + STAT + (2 * TOK if kv else 0)
    message = ((N_ULY, rows, D), BF)
    (msg,) = call(
        functools.partial(pack_kernel, first, heads, bool(kv)),
        [(array, pltpu.HBM) for array in (queries, grads, outputs, lse) + kv],
        ((message, pltpu.HBM),),
        [
            pltpu.VMEM(*message),
            pltpu.VMEM((N_ULY, TOK, heads * D), BF),
            pltpu.VMEM(lse.shape, F32),
            pltpu.SemaphoreType.DMA((4, N_ULY)),
        ],
        1,
        "pack_heads_%d" % first,
    )
    return msg


def slots_of(order_ref):
    slot = lax.axis_index("blk")
    prev = lax.rem(slot + 15, 16)
    a, b = order_ref[0, slot], order_ref[1, slot]
    pa, pb = order_ref[0, prev], order_ref[1, prev]
    low = (a > b).astype(jnp.int32)
    prev_low = (pa > pb).astype(jnp.int32)
    lower_sees = jnp.minimum(a, b) > jnp.minimum(pa, pb)
    return low, prev_low, lower_sees


def half(ref, which, at):
    return ref[pl.ds(which * 4, 4), at : at + TOK, :].reshape(HALF, D)


def tile(rows, k, v, heads=None):
    q, do, lse, delta = rows
    probs = jnp.exp2(nt(k, q) * (FACTOR * LOG2E) - lse)
    if heads is not None:
        key = lax.broadcasted_iota(jnp.int32, probs.shape, 0)
        row = lax.broadcasted_iota(jnp.int32, probs.shape, 1) % (probs.shape[1] // heads)
        probs = jnp.where(row >= key, probs, 0.0)
    d_scores = (probs * (nt(v, do) - delta) * FACTOR).astype(BF)
    return nn(probs.astype(BF), do), nn(d_scores, q), tn(d_scores, k)


def stat_rows(x_ref, at):
    blocks = []
    for s in range(N_ULY):
        p = x_ref[s, at : at + STAT, :].astype(F32)
        blocks.append(p[0:8] + p[8:16] + p[16:24])
    return jnp.concatenate(blocks, axis=1)


def pick(stats, row, which):
    lower, upper = stats[row : row + 1, :HALF], stats[row : row + 1, HALF:]
    return jnp.where(which == 0, lower, upper)


def rows_of(x_ref, stats, heads, which):
    def join(at):
        return jnp.concatenate([half(x_ref, which, (at + j) * TOK) for j in range(heads)], axis=0)

    def join_stats(at):
        return jnp.concatenate([pick(stats, at + j, which) for j in range(heads)], axis=1)

    return join(0), join(heads), join_stats(0), join_stats(heads)


def upper_rows(rows, heads):
    q, do, lse, delta = rows
    q, do = [
        jnp.concatenate([a[j * HALF + 256 : (j + 1) * HALF] for j in range(heads)], 0)
        for a in (q, do)
    ]
    lse, delta = [
        jnp.concatenate([a[:, j * HALF + 256 : (j + 1) * HALF] for j in range(heads)], 1)
        for a in (lse, delta)
    ]
    return q, do, lse, delta


def diagonal(rows, k, v, heads):
    dv0, dk0, dq0 = tile(rows, k[:256], v[:256], heads)
    dv1, dk1, dq1 = tile(upper_rows(rows, heads), k[256:], v[256:], heads)
    dq = []
    for j in range(heads):
        at = j * HALF
        dq.append(dq0[at : at + 256])
        dq.append(dq0[at + 256 : at + HALF] + dq1[j * 256 : (j + 1) * 256])
    return (
        jnp.concatenate([dv0, dv1], 0),
        jnp.concatenate([dk0, dk1], 0),
        jnp.concatenate(dq, 0),
    )


def blocks(value):
    return value.reshape(4, TOK, D)


def put(ref, index, which, value, add=False):
    at = (index, pl.ds(which * 4, 4))
    ref[at] = ref[at] + blocks(value) if add else blocks(value)


def put_heads(ref, heads, which, value, add=False):
    for j in range(heads):
        put(ref, j, which, value[j * HALF : (j + 1) * HALF], add)


def local_tiles(low, x_ref, stats, heads, k_ref, k_at, dq, dkv, after_high):
    high = 1 - low
    k_low, v_low = half(k_ref, low, k_at), half(k_ref, low, k_at + TOK)
    k_high, v_high = half(k_ref, high, k_at), half(k_ref, high, k_at + TOK)
    rows_high = rows_of(x_ref, stats, heads, high)
    rows_low = rows_of(x_ref, stats, heads, low)
    dv2, dk2, dq2 = diagonal(rows_high, k_high, v_high, heads)
    put(dkv, 0, high, dk2)
    put(dkv, 1, high, dv2)
    after_high(high)
    dv, dk, dq1 = tile(rows_high, k_low, v_low)
    put_heads(dq, heads, high, dq1 + dq2)
    dv3, dk3, dq3 = diagonal(rows_low, k_low, v_low, heads)
    put(dkv, 0, low, dk + dk3)
    put(dkv, 1, low, dv + dv3)
    put_heads(dq, heads, low, dq3)


def cross_tiles(low, prev_low, lower_sees, x_ref, stats, heads, kp_ref, dq, dkv):
    high, prev_high = 1 - low, 1 - prev_low
    k, v = half(kp_ref, prev_low, 0), half(kp_ref, prev_low, TOK)
    dv, dk, dq_high = tile(rows_of(x_ref, stats, heads, high), k, v)
    put(dkv, 0, prev_low, dk)
    put(dkv, 1, prev_low, dv)
    put_heads(dq, heads, high, dq_high)
    dkv[:, pl.ds(prev_high * 4, 4)] = jnp.zeros((2, 4, TOK, D), F32)
    dq[:, pl.ds(low * 4, 4)] = jnp.zeros((heads, 4, TOK, D), F32)
    sees = lower_sees.astype(jnp.int32)
    rows_at = sees * low + (1 - sees) * high
    keys_at = sees * prev_low + (1 - sees) * prev_high
    k, v = half(kp_ref, keys_at, 0), half(kp_ref, keys_at, TOK)
    dv, dk, dq_two = tile(rows_of(x_ref, stats, heads, rows_at), k, v)
    put(dkv, 0, keys_at, dk, True)
    put(dkv, 1, keys_at, dv, True)
    put_heads(dq, heads, rows_at, dq_two, True)


def local0_kernel(heads, order_ref, x_hbm, x_ref, dq_out, local_hbm, dkv, sem):
    low, _, _ = slots_of(order_ref)
    load = copy_of(x_hbm, x_ref, sem.at[0])
    load.start()
    load.wait()
    kv_at = 2 * heads * TOK
    stats = stat_rows(x_ref, kv_at + 2 * TOK)

    def store(which, number):
        part = pl.ds(which * 4, 4)
        return copy_of(dkv.at[:, part], local_hbm.at[:, part], sem.at[number])

    local_tiles(
        low, x_ref, stats, heads, x_ref, kv_at, dq_out, dkv, lambda high: store(high, 1).start()
    )
    store(low, 2).start()
    store(1 - low, 1).wait()
    store(low, 2).wait()


def cross0_kernel(heads, order_ref, x_ref, kp_ref, dq_in, msg_hbm, cross_hbm, dq, dkv, out, sem):
    low, prev_low, lower_sees = slots_of(order_ref)
    stats = stat_rows(x_ref, (2 * heads + 2) * TOK)
    cross_tiles(low, prev_low, lower_sees, x_ref, stats, heads, kp_ref, dq, dkv)
    store = copy_of(dkv, cross_hbm, sem.at[0])
    store.start()
    for j in range(heads):
        out[:, j * TOK : (j + 1) * TOK, :] = (dq[j] + dq_in[j]).astype(BF)
    send = copy_of(out, msg_hbm.at[:, pl.ds(0, heads * TOK), :], sem.at[1])
    send.start()
    store.wait()
    send.wait()


def cross1_kernel(
    heads, order_ref, x_hbm, kp_ref, cross_hbm, dq_hbm, cross_out, x_ref, dq, dkv, held, sem
):
    low, prev_low, lower_sees = slots_of(order_ref)
    load = copy_of(x_hbm, x_ref, sem.at[0])
    held_load = copy_of(cross_hbm, held, sem.at[1])
    load.start()
    held_load.start()
    load.wait()
    stats = stat_rows(x_ref, 2 * heads * TOK)
    cross_tiles(low, prev_low, lower_sees, x_ref, stats, heads, kp_ref, dq, dkv)
    store = copy_of(dq, dq_hbm, sem.at[2])
    store.start()
    held_load.wait()
    cross_out[...] = (dkv[...] + held[...]).astype(BF)
    store.wait()


def local1_kernel(
    heads, kv_at, order_ref, x_hbm, x0_hbm, dq_hbm, local_hbm, msg_in, msg_hbm, local_out,
    x_ref, kv_ref, dq, dq_held, held, out, sem,
):
    del msg_in
    low, _, _ = slots_of(order_ref)
    load = copy_of(x_hbm, x_ref, sem.at[0])
    kv_load = copy_of(x0_hbm.at[:, pl.ds(kv_at, 2 * TOK), :], kv_ref, sem.at[1])
    dq_load = copy_of(dq_hbm, dq_held, sem.at[2])
    held_load = copy_of(local_hbm, held, sem.at[3])
    for one in (load, kv_load, dq_load, held_load):
        one.start()
    load.wait()
    kv_load.wait()
    stats = stat_rows(x_ref, 2 * heads * TOK)
    local_tiles(low, x_ref, stats, heads, kv_ref, 0, dq, local_out, lambda high: None)
    dq_load.wait()
    for j in range(heads):
        out[:, j * TOK : (j + 1) * TOK, :] = (dq[j] + dq_held[j]).astype(BF)
    send = copy_of(out, msg_hbm.at[:, pl.ds(heads * TOK, heads * TOK), :], sem.at[4])
    send.start()
    held_load.wait()
    local_out[...] += held[...]
    send.wait()


def add_kernel(heads, local_ref, back_ref, msg_in, msg_hbm, out, sem):
    del msg_in
    for i in range(2):
        total = local_ref[i] + back_ref[i].astype(F32)
        out[:, i * TOK : (i + 1) * TOK, :] = total.astype(BF)
    send = copy_of(out, msg_hbm.at[:, pl.ds(2 * heads * TOK, 2 * TOK), :], sem.at[0])
    send.start()
    send.wait()


def unpack_kernel(x_hbm, dq_ref, dk_ref, dv_ref, buf, in_sem, sem):
    loads = [copy_of(x_hbm.at[u], buf.at[u], in_sem.at[u]) for u in range(N_ULY)]
    for load in loads:
        load.start()

    def store(u, at, target, column, which):
        cols = pl.ds(pl.multiple_of(column * D, D), D)
        copy_of(buf.at[u, pl.ds(at, TOK), :], target.at[:, cols], sem.at[which]).start()

    for u in range(N_ULY):
        group = head_group(u)
        loads[u].wait()
        for j in range(GROUP):
            store(u, j * TOK, dq_ref, group * GROUP + j, 0)
        store(u, GROUP * TOK, dk_ref, group, 1)
        store(u, (GROUP + 1) * TOK, dv_ref, group, 2)
    for which, ref in enumerate((dq_ref, dk_ref, dv_ref)):
        copy_of(ref, ref, sem.at[which]).wait()


def params():
    return pltpu.CompilerParams(vmem_limit_bytes=32 * MIB)


def shift_slot(value, by):
    pairs = []
    for slot in range(16):
        other = (slot + by) % 16
        flip = 1 if slot // 8 != other // 8 else 0
        pairs += [(slot * N_ULY + u, other * N_ULY + (u ^ flip)) for u in range(N_ULY)]
    return lax.ppermute(value, ("blk", "uly"), pairs)


def exchange(value):
    return lax.all_to_all(value, "uly", split_axis=0, concat_axis=0, tiled=True)


def call(kernel, inputs, outs, scratch, units, name, aliases=None):
    def placed(array, space):
        return pltpu.with_memory_space_constraint(array, space) if space == pltpu.HBM else array

    def shaped(shape, space):
        return pltpu.HBM(*shape) if space == pltpu.HBM else jax.ShapeDtypeStruct(*shape)

    return pl.pallas_call(
        kernel,
        in_specs=[pl.BlockSpec(memory_space=space) for _, space in inputs],
        out_specs=[pl.BlockSpec(memory_space=space) for _, space in outs],
        out_shape=[shaped(shape, space) for shape, space in outs],
        scratch_shapes=scratch,
        input_output_aliases=aliases or {},
        compiler_params=params(),
        cost_estimate=pl.CostEstimate(
            flops=units * 5 * 2 * 512 * 512 * 128 * 2,
            bytes_accessed=4 * MIB,
            transcendentals=units * 512 * 512,
        ),
        name=name,
    )(*[placed(array, space) for array, space in inputs])


def body(queries, input_keys, input_values, outputs, output_gradient, saved_logsumexp, span_order):
    h = 2
    kv_at = 2 * h * TOK
    rows4 = (N_ULY, TOK, D)
    lse = saved_logsumexp.T
    order = (span_order.T, pltpu.SMEM)
    msg0 = pack(queries, output_gradient, outputs, lse, (input_keys, input_values), 0, h)
    x0 = exchange(msg0)
    msg1 = pack(queries, output_gradient, outputs, lse, (), h, h)
    x0, msg1 = lax.optimization_barrier((x0, msg1))
    x1 = exchange(msg1)
    kv_prev = shift_slot(x0[:, kv_at : kv_at + 2 * TOK, :], 1)

    vmem, hbm = pltpu.VMEM, pltpu.HBM
    head_sums = ((h,) + rows4, F32)
    pair_sums = ((2,) + rows4, F32)
    pair_low = ((2,) + rows4, BF)
    head_low = ((N_ULY, h * TOK, D), BF)
    message = ((N_ULY, (GROUP + 2) * TOK, D), BF)
    sems = pltpu.SemaphoreType.DMA((5,))
    x0_near, dq0, local = call(
        functools.partial(local0_kernel, h),
        (order, (x0, hbm)),
        (((x0.shape, BF), vmem), (head_sums, vmem), (pair_sums, hbm)),
        [pltpu.VMEM(*pair_sums), sems],
        3 * h,
        "local_first",
    )
    msg, cross = call(
        functools.partial(cross0_kernel, h),
        (order, (x0_near, vmem), (kv_prev, vmem), (dq0, vmem)),
        ((message, hbm), (pair_sums, hbm)),
        [pltpu.VMEM(*head_sums), pltpu.VMEM(*pair_sums), pltpu.VMEM(*head_low), sems],
        2 * h,
        "cross_first",
    )
    dq1, cross_low = call(
        functools.partial(cross1_kernel, h),
        (order, (x1, hbm), (kv_prev, vmem), (cross, hbm)),
        ((head_sums, hbm), (pair_low, vmem)),
        [
            pltpu.VMEM(x1.shape, BF),
            pltpu.VMEM(*head_sums),
            pltpu.VMEM(*pair_sums),
            pltpu.VMEM(*pair_sums),
            sems,
        ],
        2 * h,
        "cross_last",
    )
    back = shift_slot(cross_low, -1)
    msg, local = call(
        functools.partial(local1_kernel, h, kv_at),
        (order, (x1, hbm), (x0, hbm), (dq1, hbm), (local, hbm), (msg, hbm)),
        ((message, hbm), (pair_sums, vmem)),
        [
            pltpu.VMEM(x1.shape, BF),
            pltpu.VMEM((N_ULY, 2 * TOK, D), BF),
            pltpu.VMEM(*head_sums),
            pltpu.VMEM(*head_sums),
            pltpu.VMEM(*pair_sums),
            pltpu.VMEM(*head_low),
            sems,
        ],
        3 * h,
        "local_last",
        {5: 0},
    )
    (msg,) = call(
        functools.partial(add_kernel, h),
        ((local, vmem), (back, vmem), (msg, hbm)),
        ((message, hbm),),
        [pltpu.VMEM((N_ULY, 2 * TOK, D), BF), sems],
        0,
        "add_returned",
        {2: 0},
    )
    result = exchange(msg)
    return call(
        unpack_kernel,
        ((result, hbm),),
        (
            (((TOK, N_ULY * GROUP * D), BF), hbm),
            (((TOK, N_ULY * D), BF), hbm),
            (((TOK, N_ULY * D), BF), hbm),
        ),
        [
            pltpu.VMEM(*message),
            pltpu.SemaphoreType.DMA((N_ULY,)),
            pltpu.SemaphoreType.DMA((3,)),
        ],
        0,
        "unpack",
    )


def solution(mesh):
    rows = P(("blk", "uly"), None)
    return jax.shard_map(
        body, mesh=mesh, in_specs=(rows,) * 6 + (P(),), out_specs=(rows,) * 3, check_vma=False
    )
```

time: 195 us -> 99.8 us (0.51)
  matrix products: 72.9 us -> 0 us
  starting transfers between devices: 45.8 us -> 9.65 us
  Pallas kernels: 0 us -> 33.9 us
  blocking collectives: 0 us -> 28.6 us
  waiting for transfers between devices: 46 us -> 25.3 us
  local copies, waits for them, and re-layouts: 21.4 us -> 1.05 us
  other arithmetic: 4.61 us -> 0 us
  between operations: 3.39 us -> 0.94 us
    dot_general x10 -> x0, matrix products: 72.9 us -> none  [the longest x2 21.8 us: tile_grads(): jnp.einsum('rkgd,ckd->kgrc', gradient_per_head, value_per_head, preferred...]
    all_to_all x9 -> x2, starting transfers between devices: 44.2 us -> 9.1 us  [exchange(): return lax.all_to_all(value, 'uly', split_axis=0, concat_axis=0, tiled=True)]
    pallas_call x0 -> x8, Pallas kernels: none -> 33.9 us  [call(): pl.pallas_call(kernel, in_specs=[pl.BlockSpec(memory_space=space) for _,...]
    all_to_all x0 -> x1, blocking collectives: none -> 28.6 us  [exchange(): return lax.all_to_all(value, 'uly', split_axis=0, concat_axis=0, tiled=True)]
    all_to_all x9 -> x2, waiting for transfers between devices: 46 us -> 21.2 us  [exchange(): return lax.all_to_all(value, 'uly', split_axis=0, concat_axis=0, tiled=True)]
    unnamed x17 -> x6, local copies, waits for them, and re-layouts: 9.39 us -> 1.02 us
    all_to_all x6 -> x0, local copies, waits for them, and re-layouts: 5.29 us -> none  [the longest x1 1.7 us: body(): lax.all_to_all(input_values, 'uly', split_axis=1, concat_axis=0, tiled=True)]
    convert_element_type x4 -> x0, local copies, waits for them, and re-layouts: 4.41 us -> none  [the longest x2 2.74 us: row_deltas(): product = output_gradient.astype(jnp.float32) * outputs.astype(jnp.float32)]
  transfers between devices with their start and end apart: 13 -> 4, of which waited for: 7 -> 2; matrix products, arithmetic and copies ran while one was open for 41% -> 0% of each run, Pallas kernels for 0% -> 21%
where the time goes in v2:
time: 99.8 us; the launch traced here: 99.3 us
  Pallas kernels  33.9 us (34%)
  blocking collectives  28.6 us (29%)
  waiting for transfers between devices  25.3 us (25%)
  starting transfers between devices  9.65 us (10%)
  local copies, waits for them, and re-layouts  1.05 us (1%)
    pallas_call x8, Pallas kernels, call(): pl.pallas_call(kernel, in_specs=[pl.BlockSpec(memory_space=space) for _,...  33.9 us
    all_to_all x1, blocking collectives, exchange(): return lax.all_to_all(value, 'uly', split_axis=0, concat_axis=0, tiled=True)  28.6 us
    all_to_all x2, waiting for transfers between devices, exchange(): return lax.all_to_all(value, 'uly', split_axis=0, concat_axis=0, tiled=True)  21.2 us
    all_to_all x2, starting transfers between devices, exchange(): return lax.all_to_all(value, 'uly', split_axis=0, concat_axis=0, tiled=True)  9.1 us
    ppermute x2, waiting for transfers between devices, shift_slot(): return lax.ppermute(value, ('blk', 'uly'), pairs)  4.11 us
  transfers between devices with their start and end apart: 4, of which 2 were waited for; matrix products, arithmetic and copies ran while one was open for 0% of the time, Pallas kernels for 21%

profile of v2, /device:TPU:64, one launch (start us, length us, event | category | flops | bytes accessed | tf_op | source)
XLA Modules:
  0.0 99.3 jit_solution(11550358515549222806)
XLA Ops:
  0.6 3.5 %pack_heads_0.1 = bf16[8,800,128]{2,1,0:T(8,128)(2,1)} custom-call(bf16[128,4096]{1,0:T(8,128)(2,1)} %refs_0_.3, bf16[128,4096]{1,0:T(8,128)(2,1)} %refs_1_.3, bf16[128,4096]{1,0:T(8,128)(2,1)} %refs_2_.3, f32[32,128]{1,0:T(8,128)} %bitcast.6, bf16[128,1024]{1,0:T(8,128)(2,1)} %refs_4_.1, bf16[128,1024]{1,0:T(8,128)(2,1)} %refs_5_.1), custom_call_target="tpu_custom_call" | custom-call | flops 671088640 | bytes 4194304 | tf_op jit(solution)/shard_map/pack_heads_0/pallas_call | solution.py:376
  4.1 5.5 %all-to-all-start = ((bf16[8,800,128]{2,1,0:T(8,128)(2,1)}), bf16[8,800,128]{2,1,0:T(8,128)(2,1)S(1)}, u32[]{:S(2)}, u32[]{:S(2)}) async-start(bf16[8,800,128]{2,1,0:T(8,128)(2,1)} %pack_heads_0.1), calls=%async_computation | async-start | bytes 3276800 | tf_op jit(solution)/shard_map/all_to_all | solution.py:366
  9.7 3.4 %pack_heads_2.1 = bf16[8,544,128]{2,1,0:T(8,128)(2,1)} custom-call(bf16[128,4096]{1,0:T(8,128)(2,1)} %refs_0_.3, bf16[128,4096]{1,0:T(8,128)(2,1)} %refs_1_.3, bf16[128,4096]{1,0:T(8,128)(2,1)} %refs_2_.3, f32[32,128]{1,0:T(8,128)} %bitcast.7), custom_call_target="tpu_custom_call" | custom-call | flops 671088640 | bytes 4194304 | tf_op jit(solution)/shard_map/pack_heads_2/pallas_call | solution.py:376
  13.1 0.0 copy-start
  13.1 21.2 %all-to-all-done.x_hbm.x0_hbm = bf16[8,800,128]{2,1,0:T(8,128)(2,1)S(1)} async-done(((bf16[8,800,128]{2,1,0:T(8,128)(2,1)}), bf16[8,800,128]{2,1,0:T(8,128)(2,1)S(1)}, u32[]{:S(2)}, u32[]{:S(2)}) %all-to-all-start) | async-done | bytes 1638432 | tf_op jit(solution)/shard_map/all_to_all | solution.py:366
  34.2 0.0 copy-start.1
  34.2 3.6 %all-to-all-start.1 = ((bf16[8,544,128]{2,1,0:T(8,128)(2,1)}), bf16[8,544,128]{2,1,0:T(8,128)(2,1)S(1)}, u32[]{:S(2)}, u32[]{:S(2)}) async-start(bf16[8,544,128]{2,1,0:T(8,128)(2,1)} %pack_heads_2.1), calls=%async_computation.1 | async-start | bytes 2228224 | tf_op jit(solution)/shard_map/all_to_all | solution.py:366
  37.9 0.0 copy-done.1
  37.9 0.3 collective-permute-start
  38.1 0.0 copy-done
  38.1 6.6 %local_first.1 = (bf16[8,800,128]{2,1,0:T(8,128)(2,1)S(1)}, f32[2,8,128,128]{3,2,1,0:T(8,128)S(1)}, f32[2,8,128,128]{3,2,1,0:T(8,128)}) custom-call(s32[2,16]{1,0:T(2,128)S(1)} %bitcast.2, bf16[8,800,128]{2,1,0:T(8,128)(2,1)} %copy-done.1), custom_call_target="tpu_custom_call" | custom-call | flops 4026531840 | bytes 4194304 | tf_op jit(solution)/shard_map/local_first/pallas_call | solution.py:376
  44.7 4.1 %collective-permute-done.kp_ref = bf16[8,256,128]{2,1,0:T(8,128)(2,1)S(1)} collective-permute-done((bf16[8,256,128]{2,1,0:T(8,128)(2,1)S(1)}, bf16[8,256,128]{2,1,0:T(8,128)(2,1)S(1)}, u32[]{:S(2)}, u32[]{:S(2)}) %collective-permute-start) | collective-permute-done | bytes 524320 | tf_op jit(solution)/shard_map/ppermute | solution.py:362
  48.8 4.7 %cross_first.1 = (bf16[8,768,128]{2,1,0:T(8,128)(2,1)}, f32[2,8,128,128]{3,2,1,0:T(8,128)}) custom-call(s32[2,16]{1,0:T(2,128)S(1)} %bitcast.3, bf16[8,800,128]{2,1,0:T(8,128)(2,1)S(1)} %get-tuple-element.16.x_ref, bf16[8,256,128]{2,1,0:T(8,128)(2,1)S(1)} %collective-permute-done.kp_ref, f32[2,8,128,128]{3,2,1,0:T(8,128)S(1)} %get-tuple-element.17.dq_in), custom_call_target="tpu_custom_call" | custom-call | flops 2684354560 | bytes 4194304 | tf_op jit(solution)/shard_map/cross_first/pallas_call | solution.py:376
  53.5 0.0 all-to-all-done.1.x_hbm
  53.5 0.0 copy-start.2
  53.6 1.0 %copy-done.2 = bf16[8,544,128]{2,1,0:T(8,128)(2,1)} copy-done((bf16[8,544,128]{2,1,0:T(8,128)(2,1)}, bf16[8,544,128]{2,1,0:T(8,128)(2,1)S(1)}, u32[]{:S(2)}) %copy-start.2) | copy-done | bytes 1114136
  54.6 5.8 %cross_last.1 = (f32[2,8,128,128]{3,2,1,0:T(8,128)}, bf16[2,8,128,128]{3,2,1,0:T(8,128)(2,1)S(1)}) custom-call(s32[2,16]{1,0:T(2,128)S(1)} %bitcast.4, bf16[8,544,128]{2,1,0:T(8,128)(2,1)} %copy-done.2, bf16[8,256,128]{2,1,0:T(8,128)(2,1)S(1)} %collective-permute-done.kp_ref, f32[2,8,128,128]{3,2,1,0:T(8,128)} %get-tuple-element.18.cross_hbm), custom_call_target="tpu_custom_call" | custom-call | flops 2684354560 | bytes 4194304 | tf_op jit(solution)/shard_map/cross_last/pallas_call | solution.py:376
  60.4 0.3 collective-permute-start.1
  60.7 6.7 %local_last.1 = (bf16[8,768,128]{2,1,0:T(8,128)(2,1)}, f32[2,8,128,128]{3,2,1,0:T(8,128)S(1)}) custom-call(s32[2,16]{1,0:T(2,128)S(1)} %bitcast.5, bf16[8,544,128]{2,1,0:T(8,128)(2,1)} %copy-done.2, bf16[8,800,128]{2,1,0:T(8,128)(2,1)} %copy-done.1, f32[2,8,128,128]{3,2,1,0:T(8,128)} %get-tuple-element.19.dq_hbm, ...), custom_call_target="tpu_custom_call", output_to_operand_aliasing={{0}: (5, {})} | custom-call | flops 4026531840 | bytes 4194304 | tf_op jit(solution)/shard_map/local_last/pallas_call | solution.py:376
  67.4 0.0 collective-permute-done.1.back_ref
  67.4 1.0 add_returned.1
  68.4 28.6 %all_to_all.15.x_hbm = bf16[8,768,128]{2,1,0:T(8,128)(2,1)} all-to-all(bf16[8,768,128]{2,1,0:T(8,128)(2,1)} %add_returned.1), channel_id=1, replica_groups=mesh['blk'=16,'uly'=8] {'uly'}, dimensions={0} | all-to-all | bytes 3145728 | tf_op jit(solution)/shard_map/all_to_all | solution.py:366
  96.9 2.2 %unpack.1 = (bf16[128,4096]{1,0:T(8,128)(2,1)}, bf16[128,1024]{1,0:T(8,128)(2,1)}, bf16[128,1024]{1,0:T(8,128)(2,1)}) custom-call(bf16[8,768,128]{2,1,0:T(8,128)(2,1)} %all_to_all.15.x_hbm), custom_call_target="tpu_custom_call" | custom-call | bytes 4194304 | tf_op jit(solution)/shard_map/unpack/pallas_call | solution.py:376
  (1 shorter events, 0.0 us)
Async XLA Ops:
  4.1 30.1 %all-to-all-start = ((bf16[8,800,128]{2,1,0:T(8,128)(2,1)}), bf16[8,800,128]{2,1,0:T(8,128)(2,1)S(1)}, u32[]{:S(2)}, u32[]{:S(2)}) async-start(bf16[8,800,128]{2,1,0:T(8,128)(2,1)} %pack_heads_0.1), calls=%async_computation | async-start | bytes 3276800 | tf_op jit(solution)/shard_map/all_to_all | solution.py:366
  13.1 25.1 %copy-start = (s32[16,2]{0,1:T(2,128)S(1)}, s32[16,2]{0,1:T(2,128)}, u32[]{:S(2)}) copy-start(s32[16,2]{0,1:T(2,128)} %param.13) | copy-start | bytes 388
  34.2 3.6 %copy-start.1 = (bf16[8,800,128]{2,1,0:T(8,128)(2,1)}, bf16[8,800,128]{2,1,0:T(8,128)(2,1)S(1)}, u32[]{:S(2)}) copy-start(bf16[8,800,128]{2,1,0:T(8,128)(2,1)S(1)} %all-to-all-done.x_hbm.x0_hbm) | copy-start | bytes 4915204
  34.2 19.3 %all-to-all-start.1 = ((bf16[8,544,128]{2,1,0:T(8,128)(2,1)}), bf16[8,544,128]{2,1,0:T(8,128)(2,1)S(1)}, u32[]{:S(2)}, u32[]{:S(2)}) async-start(bf16[8,544,128]{2,1,0:T(8,128)(2,1)} %pack_heads_2.1), calls=%async_computation.1 | async-start | bytes 2228224 | tf_op jit(solution)/shard_map/all_to_all | solution.py:366
  37.9 11.0 %collective-permute-start = (bf16[8,256,128]{2,1,0:T(8,128)(2,1)S(1)}, bf16[8,256,128]{2,1,0:T(8,128)(2,1)S(1)}, u32[]{:S(2)}, u32[]{:S(2)}) collective-permute-start(bf16[8,256,128]{2,1,0:T(8,128)(2,1)S(1)} %slice.3), channel_id=1, source_target_pairs={{0,8},{1,9},{2,10},{3,11},{4,12},{5,13},{6,14},{7,15},{8,16},{9,17... | collective-permute-start | bytes 1572872 | tf_op jit(solution)/shard_map/ppermute | solution.py:362
  53.5 1.0 %copy-start.2 = (bf16[8,544,128]{2,1,0:T(8,128)(2,1)}, bf16[8,544,128]{2,1,0:T(8,128)(2,1)S(1)}, u32[]{:S(2)}) copy-start(bf16[8,544,128]{2,1,0:T(8,128)(2,1)S(1)} %all-to-all-done.1.x_hbm) | copy-start | bytes 3342340
  60.4 7.0 %collective-permute-start.1 = (bf16[2,8,128,128]{3,2,1,0:T(8,128)(2,1)S(1)}, bf16[2,8,128,128]{3,2,1,0:T(8,128)(2,1)S(1)}, u32[]{:S(2)}, u32[]{:S(2)}) collective-permute-start(bf16[2,8,128,128]{3,2,1,0:T(8,128)(2,1)S(1)} %get-tuple-element.23), channel_id=1, source_target_pairs={{0,121},{1,120},{2,123},{3,122},{4,125},{5,124},{6,127},{7,126},{8... | collective-permute-start | bytes 1572872 | tf_op jit(solution)/shard_map/ppermute | solution.py:362

commit v3 on v2

--- a/solution.py
+++ b/solution.py
@@ -19,6 +19,24 @@
 BF = jnp.bfloat16
 F32 = jnp.float32
 MIB = 1 << 20
+ORDERS = ((0, 2, 4, 6, 1, 3, 5, 7), (7, 6, 5, 4, 3, 2, 1, 0))
+PLACES = tuple(tuple(order.index(u) for u in range(N_ULY)) for order in ORDERS)
+
+
+def parity():
+    return lax.axis_index("blk") % 2
+
+
+def choose(table, index, odd):
+    return table[0][index] + odd * (table[1][index] - table[0][index])
+
+
+def device_at(place):
+    return choose(ORDERS, place, parity())
+
+
+def place_of(u):
+    return choose(PLACES, u, parity())
 
 
 def nt(a, b):
@@ -39,7 +57,7 @@
 
 def head_group(u):
     upper = lax.axis_index("blk") // 8
-    return u + upper * (1 - 2 * (u % 2))
+    return u ^ upper
 
 
 def pack_kernel(first, heads, with_kv, *refs):
@@ -51,8 +69,8 @@
     lse_load = copy_of(lse_hbm, lse_ref, sem.at[3, 0])
     lse_load.start()
 
-    for u in range(N_ULY):
-        group = head_group(u)
+    groups = [head_group(device_at(i)) for i in range(N_ULY)]
+    for u, group in enumerate(groups):
 
         def load(source, column, at):
             cols = pl.ds(pl.multiple_of(column * D, D), D)
@@ -73,7 +91,7 @@
         loaded = buf.at[u, pl.ds(0, rows), :]
         copy_of(loaded, loaded, sem.at[0, u]).wait()
         copy_of(o_buf.at[u], o_buf.at[u], sem.at[1, u]).wait()
-        at = head_group(u) * GROUP + first
+        at = groups[u] * GROUP + first
         stats = jnp.zeros((8, TOK), F32)
         for j in range(heads):
             grads = buf[u, (heads + j) * TOK : (heads + j + 1) * TOK, :].astype(F32)
@@ -124,8 +142,13 @@
     return low, prev_low, lower_sees
 
 
-def half(ref, which, at):
-    return ref[pl.ds(which * 4, 4), at : at + TOK, :].reshape(HALF, D)
+def half(ref, which, at, odd=None):
+    odd = parity() if odd is None else odd
+    parts = []
+    for b in range(4):
+        lower, upper = choose(PLACES, b, odd), choose(PLACES, 4 + b, odd)
+        parts.append(ref[lower + which * (upper - lower), at : at + TOK, :])
+    return jnp.concatenate(parts, axis=0)
 
 
 def tile(rows, k, v, heads=None):
@@ -142,7 +165,7 @@
 def stat_rows(x_ref, at):
     blocks = []
     for s in range(N_ULY):
-        p = x_ref[s, at : at + STAT, :].astype(F32)
+        p = x_ref[place_of(s), at : at + STAT, :].astype(F32)
         blocks.append(p[0:8] + p[8:16] + p[16:24])
     return jnp.concatenate(blocks, axis=1)
 
@@ -224,7 +247,8 @@
 
 def cross_tiles(low, prev_low, lower_sees, x_ref, stats, heads, kp_ref, dq, dkv):
     high, prev_high = 1 - low, 1 - prev_low
-    k, v = half(kp_ref, prev_low, 0), half(kp_ref, prev_low, TOK)
+    odd = 1 - parity()
+    k, v = half(kp_ref, prev_low, 0, odd), half(kp_ref, prev_low, TOK, odd)
     dv, dk, dq_high = tile(rows_of(x_ref, stats, heads, high), k, v)
     put(dkv, 0, prev_low, dk)
     put(dkv, 1, prev_low, dv)
@@ -234,18 +258,22 @@
     sees = lower_sees.astype(jnp.int32)
     rows_at = sees * low + (1 - sees) * high
     keys_at = sees * prev_low + (1 - sees) * prev_high
-    k, v = half(kp_ref, keys_at, 0), half(kp_ref, keys_at, TOK)
+    k, v = half(kp_ref, keys_at, 0, odd), half(kp_ref, keys_at, TOK, odd)
     dv, dk, dq_two = tile(rows_of(x_ref, stats, heads, rows_at), k, v)
     put(dkv, 0, keys_at, dk, True)
     put(dkv, 1, keys_at, dv, True)
     put_heads(dq, heads, rows_at, dq_two, True)
 
 
-def local0_kernel(heads, order_ref, x_hbm, x_ref, dq_out, local_hbm, dkv, sem):
+def send_rows(out, msg_hbm, at, sem):
+    rows = out.shape[1]
+    for u in range(N_ULY):
+        copy_of(out.at[u], msg_hbm.at[place_of(u), pl.ds(at, rows), :], sem).start()
+    return copy_of(out, out, sem)
+
+
+def local0_kernel(heads, order_ref, x_ref, dq_out, local_hbm, dkv, sem):
     low, _, _ = slots_of(order_ref)
-    load = copy_of(x_hbm, x_ref, sem.at[0])
-    load.start()
-    load.wait()
     kv_at = 2 * heads * TOK
     stats = stat_rows(x_ref, kv_at + 2 * TOK)
 
@@ -269,21 +297,15 @@
     store.start()
     for j in range(heads):
         out[:, j * TOK : (j + 1) * TOK, :] = (dq[j] + dq_in[j]).astype(BF)
-    send = copy_of(out, msg_hbm.at[:, pl.ds(0, heads * TOK), :], sem.at[1])
-    send.start()
+    send = send_rows(out, msg_hbm, 0, sem.at[1])
     store.wait()
     send.wait()
 
 
-def cross1_kernel(
-    heads, order_ref, x_hbm, kp_ref, cross_hbm, dq_hbm, cross_out, x_ref, dq, dkv, held, sem
-):
+def cross1_kernel(heads, order_ref, x_ref, kp_ref, cross_hbm, dq_hbm, cross_out, dq, dkv, held, sem):
     low, prev_low, lower_sees = slots_of(order_ref)
-    load = copy_of(x_hbm, x_ref, sem.at[0])
     held_load = copy_of(cross_hbm, held, sem.at[1])
-    load.start()
     held_load.start()
-    load.wait()
     stats = stat_rows(x_ref, 2 * heads * TOK)
     cross_tiles(low, prev_low, lower_sees, x_ref, stats, heads, kp_ref, dq, dkv)
     store = copy_of(dq, dq_hbm, sem.at[2])
@@ -294,26 +316,21 @@
 
 
 def local1_kernel(
-    heads, kv_at, order_ref, x_hbm, x0_hbm, dq_hbm, local_hbm, msg_in, msg_hbm, local_out,
-    x_ref, kv_ref, dq, dq_held, held, out, sem,
+    heads, kv_at, order_ref, x_ref, x0_ref, dq_hbm, local_hbm, msg_in, msg_hbm, local_out,
+    dq, dq_held, held, out, sem,
 ):
     del msg_in
     low, _, _ = slots_of(order_ref)
-    load = copy_of(x_hbm, x_ref, sem.at[0])
-    kv_load = copy_of(x0_hbm.at[:, pl.ds(kv_at, 2 * TOK), :], kv_ref, sem.at[1])
     dq_load = copy_of(dq_hbm, dq_held, sem.at[2])
     held_load = copy_of(local_hbm, held, sem.at[3])
-    for one in (load, kv_load, dq_load, held_load):
-        one.start()
-    load.wait()
-    kv_load.wait()
+    dq_load.start()
+    held_load.start()
     stats = stat_rows(x_ref, 2 * heads * TOK)
-    local_tiles(low, x_ref, stats, heads, kv_ref, 0, dq, local_out, lambda high: None)
+    local_tiles(low, x_ref, stats, heads, x0_ref, kv_at, dq, local_out, lambda high: None)
     dq_load.wait()
     for j in range(heads):
         out[:, j * TOK : (j + 1) * TOK, :] = (dq[j] + dq_held[j]).astype(BF)
-    send = copy_of(out, msg_hbm.at[:, pl.ds(heads * TOK, heads * TOK), :], sem.at[4])
-    send.start()
+    send = send_rows(out, msg_hbm, heads * TOK, sem.at[4])
     held_load.wait()
     local_out[...] += held[...]
     send.wait()
@@ -324,9 +341,7 @@
     for i in range(2):
         total = local_ref[i] + back_ref[i].astype(F32)
         out[:, i * TOK : (i + 1) * TOK, :] = total.astype(BF)
-    send = copy_of(out, msg_hbm.at[:, pl.ds(2 * heads * TOK, 2 * TOK), :], sem.at[0])
-    send.start()
-    send.wait()
+    send_rows(out, msg_hbm, 2 * heads * TOK, sem.at[0]).wait()
 
 
 def unpack_kernel(x_hbm, dq_ref, dk_ref, dv_ref, buf, in_sem, sem):
@@ -339,7 +354,7 @@
         copy_of(buf.at[u, pl.ds(at, TOK), :], target.at[:, cols], sem.at[which]).start()
 
     for u in range(N_ULY):
-        group = head_group(u)
+        group = head_group(device_at(u))
         loads[u].wait()
         for j in range(GROUP):
             store(u, j * TOK, dq_ref, group * GROUP + j, 0)
@@ -363,7 +378,10 @@
 
 
 def exchange(value):
-    return lax.all_to_all(value, "uly", split_axis=0, concat_axis=0, tiled=True)
+    groups = [[b * N_ULY + u for u in ORDERS[b % 2]] for b in range(16)]
+    return lax.all_to_all(
+        value, ("blk", "uly"), split_axis=0, concat_axis=0, axis_index_groups=groups, tiled=True
+    )
 
 
 def call(kernel, inputs, outs, scratch, units, name, aliases=None):
@@ -410,17 +428,17 @@
     head_low = ((N_ULY, h * TOK, D), BF)
     message = ((N_ULY, (GROUP + 2) * TOK, D), BF)
     sems = pltpu.SemaphoreType.DMA((5,))
-    x0_near, dq0, local = call(
+    dq0, local = call(
         functools.partial(local0_kernel, h),
-        (order, (x0, hbm)),
-        (((x0.shape, BF), vmem), (head_sums, vmem), (pair_sums, hbm)),
+        (order, (x0, vmem)),
+        ((head_sums, vmem), (pair_sums, hbm)),
         [pltpu.VMEM(*pair_sums), sems],
         3 * h,
         "local_first",
     )
     msg, cross = call(
         functools.partial(cross0_kernel, h),
-        (order, (x0_near, vmem), (kv_prev, vmem), (dq0, vmem)),
+        (order, (x0, vmem), (kv_prev, vmem), (dq0, vmem)),
         ((message, hbm), (pair_sums, hbm)),
         [pltpu.VMEM(*head_sums), pltpu.VMEM(*pair_sums), pltpu.VMEM(*head_low), sems],
         2 * h,
@@ -428,10 +446,9 @@
     )
     dq1, cross_low = call(
         functools.partial(cross1_kernel, h),
-        (order, (x1, hbm), (kv_prev, vmem), (cross, hbm)),
+        (order, (x1, vmem), (kv_prev, vmem), (cross, hbm)),
         ((head_sums, hbm), (pair_low, vmem)),
         [
-            pltpu.VMEM(x1.shape, BF),
             pltpu.VMEM(*head_sums),
             pltpu.VMEM(*pair_sums),
             pltpu.VMEM(*pair_sums),
@@ -443,11 +460,9 @@
     back = shift_slot(cross_low, -1)
     msg, local = call(
         functools.partial(local1_kernel, h, kv_at),
-        (order, (x1, hbm), (x0, hbm), (dq1, hbm), (local, hbm), (msg, hbm)),
+        (order, (x1, vmem), (x0, vmem), (dq1, hbm), (local, hbm), (msg, hbm)),
         ((message, hbm), (pair_sums, vmem)),
         [
-            pltpu.VMEM(x1.shape, BF),
-            pltpu.VMEM((N_ULY, 2 * TOK, D), BF),
             pltpu.VMEM(*head_sums),
             pltpu.VMEM(*head_sums),
             pltpu.VMEM(*pair_sums),

time: 99.8 us -> 94.8 us (0.950)
  waiting for transfers between devices: 25.3 us -> 21.8 us
  Pallas kernels: 33.9 us -> 30.6 us
  starting transfers between devices: 9.65 us -> 12.7 us
  local copies, waits for them, and re-layouts: 1.05 us -> 0.04 us
    all_to_all x2, waiting for transfers between devices: 21.2 us -> 17.2 us  [exchange(): lax.all_to_all(value, ('blk', 'uly'), split_axis=0, concat_axis=0, axis_i...]
    pallas_call x8, Pallas kernels: 33.9 us -> 30.6 us  [call(): pl.pallas_call(kernel, in_specs=[pl.BlockSpec(memory_space=space) for _,...]
    all_to_all x2, starting transfers between devices: 9.1 us -> 10.6 us  [exchange(): lax.all_to_all(value, ('blk', 'uly'), split_axis=0, concat_axis=0, axis_i...]
    ppermute x2, starting transfers between devices: 0.55 us -> 2.07 us  [shift_slot(): return lax.ppermute(value, ('blk', 'uly'), pairs)]
    unnamed x6 -> x2, local copies, waits for them, and re-layouts: 1.02 us -> 0.01 us
  transfers between devices with their start and end apart: 4 -> 4, of which waited for: 2 -> 3; matrix products, arithmetic and copies ran while one was open for 0% -> 0% of each run, Pallas kernels for 21% -> 21%
where the time goes in v3:
time: 94.8 us; the launch traced here: 94 us
  Pallas kernels  30.6 us (32%)
  blocking collectives  28 us (30%)
  waiting for transfers between devices  21.8 us (23%)
  starting transfers between devices  12.7 us (13%)
    pallas_call x8, Pallas kernels, call(): pl.pallas_call(kernel, in_specs=[pl.BlockSpec(memory_space=space) for _,...  30.6 us
    all_to_all x1, blocking collectives, exchange(): lax.all_to_all(value, ('blk', 'uly'), split_axis=0, concat_axis=0, axis_i...  28 us
    all_to_all x2, waiting for transfers between devices, exchange(): lax.all_to_all(value, ('blk', 'uly'), split_axis=0, concat_axis=0, axis_i...  17.2 us
    all_to_all x2, starting transfers between devices, exchange(): lax.all_to_all(value, ('blk', 'uly'), split_axis=0, concat_axis=0, axis_i...  10.6 us
    ppermute x2, waiting for transfers between devices, shift_slot(): return lax.ppermute(value, ('blk', 'uly'), pairs)  4.61 us
    ppermute x2, starting transfers between devices, shift_slot(): return lax.ppermute(value, ('blk', 'uly'), pairs)  2.07 us
  transfers between devices with their start and end apart: 4, of which 3 were waited for; matrix products, arithmetic and copies ran while one was open for 0% of the time, Pallas kernels for 21%

profile of v3, /device:TPU:64, one launch (start us, length us, event | category | flops | bytes accessed | tf_op | source)
XLA Modules:
  0.0 94.0 jit_solution(3848640654945381854)
XLA Ops:
  0.6 3.5 %pack_heads_0.1 = bf16[8,800,128]{2,1,0:T(8,128)(2,1)} custom-call(bf16[128,4096]{1,0:T(8,128)(2,1)} %refs_0_.3, bf16[128,4096]{1,0:T(8,128)(2,1)} %refs_1_.3, bf16[128,4096]{1,0:T(8,128)(2,1)} %refs_2_.3, f32[32,128]{1,0:T(8,128)} %bitcast.6, bf16[128,1024]{1,0:T(8,128)(2,1)} %refs_4_.1, bf16[128,1024]{1,0:T(8,128)(2,1)} %refs_5_.1), custom_call_target="tpu_custom_call" | custom-call | flops 671088640 | bytes 4194304 | tf_op jit(solution)/shard_map/pack_heads_0/pallas_call | solution.py:394
  4.1 5.5 %all-to-all-start = ((bf16[8,800,128]{2,1,0:T(8,128)(2,1)}), bf16[8,800,128]{2,1,0:T(8,128)(2,1)S(1)}, u32[]{:S(2)}, u32[]{:S(2)}) async-start(bf16[8,800,128]{2,1,0:T(8,128)(2,1)} %pack_heads_0.1), calls=%async_computation | async-start | bytes 3276800 | tf_op jit(solution)/shard_map/all_to_all | solution.py:382
  9.7 3.4 %pack_heads_2.1 = bf16[8,544,128]{2,1,0:T(8,128)(2,1)} custom-call(bf16[128,4096]{1,0:T(8,128)(2,1)} %refs_0_.3, bf16[128,4096]{1,0:T(8,128)(2,1)} %refs_1_.3, bf16[128,4096]{1,0:T(8,128)(2,1)} %refs_2_.3, f32[32,128]{1,0:T(8,128)} %bitcast.7), custom_call_target="tpu_custom_call" | custom-call | flops 671088640 | bytes 4194304 | tf_op jit(solution)/shard_map/pack_heads_2/pallas_call | solution.py:394
  13.1 0.0 copy-start
  13.1 17.2 %all-to-all-done.x_ref.x0_ref = bf16[8,800,128]{2,1,0:T(8,128)(2,1)S(1)} async-done(((bf16[8,800,128]{2,1,0:T(8,128)(2,1)}), bf16[8,800,128]{2,1,0:T(8,128)(2,1)S(1)}, u32[]{:S(2)}, u32[]{:S(2)}) %all-to-all-start) | async-done | bytes 1638432 | tf_op jit(solution)/shard_map/all_to_all | solution.py:382
  30.3 5.1 %all-to-all-start.1 = ((bf16[8,544,128]{2,1,0:T(8,128)(2,1)}), bf16[8,544,128]{2,1,0:T(8,128)(2,1)S(1)}, u32[]{:S(2)}, u32[]{:S(2)}) async-start(bf16[8,544,128]{2,1,0:T(8,128)(2,1)} %pack_heads_2.1), calls=%async_computation.1 | async-start | bytes 2228224 | tf_op jit(solution)/shard_map/all_to_all | solution.py:382
  35.4 1.8 %collective-permute-start = (bf16[8,256,128]{2,1,0:T(8,128)(2,1)S(1)}, bf16[8,256,128]{2,1,0:T(8,128)(2,1)S(1)}, u32[]{:S(2)}, u32[]{:S(2)}) collective-permute-start(bf16[8,256,128]{2,1,0:T(8,128)(2,1)S(1)} %slice.3), channel_id=1, source_target_pairs={{0,8},{1,9},{2,10},{3,11},{4,12},{5,13},{6,14},{7,15},{8,16},{9,17... | collective-permute-start | bytes 1572872 | tf_op jit(solution)/shard_map/ppermute | solution.py:377
  37.2 0.0 copy-done
  37.2 5.1 %local_first.1 = (f32[2,8,128,128]{3,2,1,0:T(8,128)S(1)}, f32[2,8,128,128]{3,2,1,0:T(8,128)}) custom-call(s32[2,16]{1,0:T(2,128)S(1)} %bitcast.2, bf16[8,800,128]{2,1,0:T(8,128)(2,1)S(1)} %all-to-all-done.x_ref.x0_ref), custom_call_target="tpu_custom_call" | custom-call | flops 4026531840 | bytes 4194304 | tf_op jit(solution)/shard_map/local_first/pallas_call | solution.py:394
  42.4 4.0 %collective-permute-done.kp_ref = bf16[8,256,128]{2,1,0:T(8,128)(2,1)S(1)} collective-permute-done((bf16[8,256,128]{2,1,0:T(8,128)(2,1)S(1)}, bf16[8,256,128]{2,1,0:T(8,128)(2,1)S(1)}, u32[]{:S(2)}, u32[]{:S(2)}) %collective-permute-start) | collective-permute-done | bytes 524320 | tf_op jit(solution)/shard_map/ppermute | solution.py:377
  46.4 4.7 %cross_first.1 = (bf16[8,768,128]{2,1,0:T(8,128)(2,1)}, f32[2,8,128,128]{3,2,1,0:T(8,128)}) custom-call(s32[2,16]{1,0:T(2,128)S(1)} %bitcast.3, bf16[8,800,128]{2,1,0:T(8,128)(2,1)S(1)} %all-to-all-done.x_ref.x0_ref, bf16[8,256,128]{2,1,0:T(8,128)(2,1)S(1)} %collective-permute-done.kp_ref, f32[2,8,128,128]{3,2,1,0:T(8,128)S(1)} %get-tuple-element.15.dq_in), custom_call_target="tpu_custom_call" | custom-call | flops 2684354560 | bytes 4194304 | tf_op jit(solution)/shard_map/cross_first/pallas_call | solution.py:394
  51.1 0.0 all-to-all-done.1.x_ref
  51.1 4.6 %cross_last.1 = (f32[2,8,128,128]{3,2,1,0:T(8,128)}, bf16[2,8,128,128]{3,2,1,0:T(8,128)(2,1)S(1)}) custom-call(s32[2,16]{1,0:T(2,128)S(1)} %bitcast.4, bf16[8,544,128]{2,1,0:T(8,128)(2,1)S(1)} %all-to-all-done.1.x_ref, bf16[8,256,128]{2,1,0:T(8,128)(2,1)S(1)} %collective-permute-done.kp_ref, f32[2,8,128,128]{3,2,1,0:T(8,128)} %get-tuple-element.16.cross_hbm), custom_call_target="tpu_custom_call" | custom-call | flops 2684354560 | bytes 4194304 | tf_op jit(solution)/shard_map/cross_last/pallas_call | solution.py:394
  55.7 0.3 collective-permute-start.1
  56.0 6.1 %local_last.1 = (bf16[8,768,128]{2,1,0:T(8,128)(2,1)}, f32[2,8,128,128]{3,2,1,0:T(8,128)S(1)}) custom-call(s32[2,16]{1,0:T(2,128)S(1)} %bitcast.5, bf16[8,544,128]{2,1,0:T(8,128)(2,1)S(1)} %all-to-all-done.1.x_ref, bf16[8,800,128]{2,1,0:T(8,128)(2,1)S(1)} %all-to-all-done.x_ref.x0_ref, ...), custom_call_target="tpu_custom_call", output_to_operand_aliasing={{0}: (5, {})} | custom-call | flops 4026531840 | bytes 4194304 | tf_op jit(solution)/shard_map/local_last/pallas_call | solution.py:394
  62.1 0.6 collective-permute-done.1.back_ref
  62.7 0.9 add_returned.1
  63.6 28.0 %all_to_all.15.x_hbm = bf16[8,768,128]{2,1,0:T(8,128)(2,1)} all-to-all(bf16[8,768,128]{2,1,0:T(8,128)(2,1)} %add_returned.1), channel_id=1, replica_groups={{0,2,4,6,1,3,5,7},{15,14,13,12,11,10,9,8},{16,18,20,22,17,19,21,23},{31..., dimensions={0} | all-to-all | bytes 3145728 | tf_op jit(solution)/shard_map/all_to_all | solution.py:382
  91.6 2.2 %unpack.1 = (bf16[128,4096]{1,0:T(8,128)(2,1)}, bf16[128,1024]{1,0:T(8,128)(2,1)}, bf16[128,1024]{1,0:T(8,128)(2,1)}) custom-call(bf16[8,768,128]{2,1,0:T(8,128)(2,1)} %all_to_all.15.x_hbm), custom_call_target="tpu_custom_call" | custom-call | bytes 4194304 | tf_op jit(solution)/shard_map/unpack/pallas_call | solution.py:394
  (1 shorter events, 0.0 us)
Async XLA Ops:
  4.1 26.2 %all-to-all-start = ((bf16[8,800,128]{2,1,0:T(8,128)(2,1)}), bf16[8,800,128]{2,1,0:T(8,128)(2,1)S(1)}, u32[]{:S(2)}, u32[]{:S(2)}) async-start(bf16[8,800,128]{2,1,0:T(8,128)(2,1)} %pack_heads_0.1), calls=%async_computation | async-start | bytes 3276800 | tf_op jit(solution)/shard_map/all_to_all | solution.py:382
  13.1 24.1 %copy-start = (s32[16,2]{0,1:T(2,128)S(1)}, s32[16,2]{0,1:T(2,128)}, u32[]{:S(2)}) copy-start(s32[16,2]{0,1:T(2,128)} %param.13) | copy-start | bytes 388
  30.3 20.8 %all-to-all-start.1 = ((bf16[8,544,128]{2,1,0:T(8,128)(2,1)}), bf16[8,544,128]{2,1,0:T(8,128)(2,1)S(1)}, u32[]{:S(2)}, u32[]{:S(2)}) async-start(bf16[8,544,128]{2,1,0:T(8,128)(2,1)} %pack_heads_2.1), calls=%async_computation.1 | async-start | bytes 2228224 | tf_op jit(solution)/shard_map/all_to_all | solution.py:382
  35.4 11.0 %collective-permute-start = (bf16[8,256,128]{2,1,0:T(8,128)(2,1)S(1)}, bf16[8,256,128]{2,1,0:T(8,128)(2,1)S(1)}, u32[]{:S(2)}, u32[]{:S(2)}) collective-permute-start(bf16[8,256,128]{2,1,0:T(8,128)(2,1)S(1)} %slice.3), channel_id=1, source_target_pairs={{0,8},{1,9},{2,10},{3,11},{4,12},{5,13},{6,14},{7,15},{8,16},{9,17... | collective-permute-start | bytes 1572872 | tf_op jit(solution)/shard_map/ppermute | solution.py:377
  55.7 7.0 %collective-permute-start.1 = (bf16[2,8,128,128]{3,2,1,0:T(8,128)(2,1)S(1)}, bf16[2,8,128,128]{3,2,1,0:T(8,128)(2,1)S(1)}, u32[]{:S(2)}, u32[]{:S(2)}) collective-permute-start(bf16[2,8,128,128]{3,2,1,0:T(8,128)(2,1)S(1)} %get-tuple-element.21), channel_id=1, source_target_pairs={{0,121},{1,120},{2,123},{3,122},{4,125},{5,124},{6,127},{7,126},{8... | collective-permute-start | bytes 1572872 | tf_op jit(solution)/shard_map/ppermute | solution.py:377

commit v4 on v3

--- a/solution.py
+++ b/solution.py
@@ -15,7 +15,7 @@
 HALF = 512
 FACTOR = 1.0 / math.sqrt(D)
 LOG2E = math.log2(math.e)
-STAT = 32
+STAT = 16
 BF = jnp.bfloat16
 F32 = jnp.float32
 MIB = 1 << 20
@@ -102,6 +102,7 @@
             stats = stats + nt(ones, high) + nt(ones, low)
             lse_one = lse_ref[pl.ds(at + j, 1), :] * LOG2E
             stats = stats + jnp.where(row_of == j, lse_one, 0.0)
+        stats = stats[: 2 * heads]
         p0 = stats.astype(BF).astype(F32)
         p1 = (stats - p0).astype(BF).astype(F32)
         p2 = stats - p0 - p1
@@ -151,7 +152,7 @@
     return jnp.concatenate(parts, axis=0)
 
 
-def tile(rows, k, v, heads=None):
+def key_grads(rows, k, v, heads=None):
     q, do, lse, delta = rows
     probs = jnp.exp2(nt(k, q) * (FACTOR * LOG2E) - lse)
     if heads is not None:
@@ -159,15 +160,20 @@
         row = lax.broadcasted_iota(jnp.int32, probs.shape, 1) % (probs.shape[1] // heads)
         probs = jnp.where(row >= key, probs, 0.0)
     d_scores = (probs * (nt(v, do) - delta) * FACTOR).astype(BF)
-    return nn(probs.astype(BF), do), nn(d_scores, q), tn(d_scores, k)
+    return nn(probs.astype(BF), do), nn(d_scores, q), d_scores
+
+
+def tile(rows, k, v, heads=None):
+    dv, dk, d_scores = key_grads(rows, k, v, heads)
+    return dv, dk, tn(d_scores, k)
 
 
 def stat_rows(x_ref, at):
-    blocks = []
+    parts = []
     for s in range(N_ULY):
         p = x_ref[place_of(s), at : at + STAT, :].astype(F32)
-        blocks.append(p[0:8] + p[8:16] + p[16:24])
-    return jnp.concatenate(blocks, axis=1)
+        parts.append(p[0:4] + p[4:8] + p[8:12])
+    return jnp.concatenate(parts, axis=1)
 
 
 def pick(stats, row, which):
@@ -245,24 +251,24 @@
     put_heads(dq, heads, low, dq3)
 
 
-def cross_tiles(low, prev_low, lower_sees, x_ref, stats, heads, kp_ref, dq, dkv):
-    high, prev_high = 1 - low, 1 - prev_low
+def second_tile(low, prev_low, lower_sees):
+    sees = lower_sees.astype(jnp.int32)
+    return sees * low + (1 - sees) * (1 - low), sees * prev_low + (1 - sees) * (1 - prev_low)
+
+
+def cross_tiles(low, prev_low, lower_sees, x_ref, stats, heads, kp_ref, dkv, first, second):
     odd = 1 - parity()
-    k, v = half(kp_ref, prev_low, 0, odd), half(kp_ref, prev_low, TOK, odd)
-    dv, dk, dq_high = tile(rows_of(x_ref, stats, heads, high), k, v)
-    put(dkv, 0, prev_low, dk)
-    put(dkv, 1, prev_low, dv)
-    put_heads(dq, heads, high, dq_high)
-    dkv[:, pl.ds(prev_high * 4, 4)] = jnp.zeros((2, 4, TOK, D), F32)
-    dq[:, pl.ds(low * 4, 4)] = jnp.zeros((heads, 4, TOK, D), F32)
-    sees = lower_sees.astype(jnp.int32)
-    rows_at = sees * low + (1 - sees) * high
-    keys_at = sees * prev_low + (1 - sees) * prev_high
-    k, v = half(kp_ref, keys_at, 0, odd), half(kp_ref, keys_at, TOK, odd)
-    dv, dk, dq_two = tile(rows_of(x_ref, stats, heads, rows_at), k, v)
-    put(dkv, 0, keys_at, dk, True)
-    put(dkv, 1, keys_at, dv, True)
-    put_heads(dq, heads, rows_at, dq_two, True)
+
+    def one(rows_at, keys_at, take, add):
+        k, v = half(kp_ref, keys_at, 0, odd), half(kp_ref, keys_at, TOK, odd)
+        dv, dk, d_scores = key_grads(rows_of(x_ref, stats, heads, rows_at), k, v)
+        put(dkv, 0, keys_at, dk, add)
+        put(dkv, 1, keys_at, dv, add)
+        take(rows_at, k, d_scores)
+
+    one(1 - low, prev_low, first, False)
+    dkv[:, pl.ds((1 - prev_low) * 4, 4)] = jnp.zeros((2, 4, TOK, D), F32)
+    one(*second_tile(low, prev_low, lower_sees), second, True)
 
 
 def send_rows(out, msg_hbm, at, sem):
@@ -292,7 +298,15 @@
 def cross0_kernel(heads, order_ref, x_ref, kp_ref, dq_in, msg_hbm, cross_hbm, dq, dkv, out, sem):
     low, prev_low, lower_sees = slots_of(order_ref)
     stats = stat_rows(x_ref, (2 * heads + 2) * TOK)
-    cross_tiles(low, prev_low, lower_sees, x_ref, stats, heads, kp_ref, dq, dkv)
+
+    def first(rows_at, k, d_scores):
+        put_heads(dq, heads, rows_at, tn(d_scores, k))
+        dq[:, pl.ds(low * 4, 4)] = jnp.zeros((heads, 4, TOK, D), F32)
+
+    def second(rows_at, k, d_scores):
+        put_heads(dq, heads, rows_at, tn(d_scores, k), True)
+
+    cross_tiles(low, prev_low, lower_sees, x_ref, stats, heads, kp_ref, dkv, first, second)
     store = copy_of(dkv, cross_hbm, sem.at[0])
     store.start()
     for j in range(heads):
@@ -302,34 +316,40 @@
     send.wait()
 
 
-def cross1_kernel(heads, order_ref, x_ref, kp_ref, cross_hbm, dq_hbm, cross_out, dq, dkv, held, sem):
+def cross1_kernel(heads, order_ref, x_ref, kp_ref, cross_hbm, ds_out, cross_out, dkv, held, sem):
     low, prev_low, lower_sees = slots_of(order_ref)
     held_load = copy_of(cross_hbm, held, sem.at[1])
     held_load.start()
     stats = stat_rows(x_ref, 2 * heads * TOK)
-    cross_tiles(low, prev_low, lower_sees, x_ref, stats, heads, kp_ref, dq, dkv)
-    store = copy_of(dq, dq_hbm, sem.at[2])
-    store.start()
+
+    def keep(number):
+        def take(rows_at, k, d_scores):
+            ds_out[number] = d_scores
+
+        return take
+
+    cross_tiles(low, prev_low, lower_sees, x_ref, stats, heads, kp_ref, dkv, keep(0), keep(1))
     held_load.wait()
     cross_out[...] = (dkv[...] + held[...]).astype(BF)
-    store.wait()
 
 
 def local1_kernel(
-    heads, kv_at, order_ref, x_ref, x0_ref, dq_hbm, local_hbm, msg_in, msg_hbm, local_out,
-    dq, dq_held, held, out, sem,
+    heads, kv_at, order_ref, x_ref, x0_ref, kp_ref, ds_ref, local_hbm, msg_in, msg_hbm, local_out,
+    dq, held, out, sem,
 ):
     del msg_in
-    low, _, _ = slots_of(order_ref)
-    dq_load = copy_of(dq_hbm, dq_held, sem.at[2])
+    low, prev_low, lower_sees = slots_of(order_ref)
     held_load = copy_of(local_hbm, held, sem.at[3])
-    dq_load.start()
     held_load.start()
     stats = stat_rows(x_ref, 2 * heads * TOK)
     local_tiles(low, x_ref, stats, heads, x0_ref, kv_at, dq, local_out, lambda high: None)
-    dq_load.wait()
+    odd = 1 - parity()
+    tiles = ((1 - low, prev_low), second_tile(low, prev_low, lower_sees))
+    for number, (rows_at, keys_at) in enumerate(tiles):
+        k = half(kp_ref, keys_at, 0, odd)
+        put_heads(dq, heads, rows_at, tn(ds_ref[number], k), True)
     for j in range(heads):
-        out[:, j * TOK : (j + 1) * TOK, :] = (dq[j] + dq_held[j]).astype(BF)
+        out[:, j * TOK : (j + 1) * TOK, :] = dq[j].astype(BF)
     send = send_rows(out, msg_hbm, heads * TOK, sem.at[4])
     held_load.wait()
     local_out[...] += held[...]
@@ -338,24 +358,25 @@
 
 def add_kernel(heads, local_ref, back_ref, msg_in, msg_hbm, out, sem):
     del msg_in
-    for i in range(2):
-        total = local_ref[i] + back_ref[i].astype(F32)
-        out[:, i * TOK : (i + 1) * TOK, :] = total.astype(BF)
-    send_rows(out, msg_hbm, 2 * heads * TOK, sem.at[0]).wait()
-
-
-def unpack_kernel(x_hbm, dq_ref, dk_ref, dv_ref, buf, in_sem, sem):
-    loads = [copy_of(x_hbm.at[u], buf.at[u], in_sem.at[u]) for u in range(N_ULY)]
-    for load in loads:
-        load.start()
-
+    sends = []
+    for u in range(N_ULY):
+        for i in range(2):
+            total = local_ref[i, u] + back_ref[i, u].astype(F32)
+            out[u, i * TOK : (i + 1) * TOK, :] = total.astype(BF)
+        rows = pl.ds(2 * heads * TOK, 2 * TOK)
+        sends.append(copy_of(out.at[u], msg_hbm.at[place_of(u), rows, :], sem.at[u]))
+        sends[u].start()
+    for send in sends:
+        send.wait()
+
+
+def unpack_kernel(x_ref, dq_ref, dk_ref, dv_ref, sem):
     def store(u, at, target, column, which):
         cols = pl.ds(pl.multiple_of(column * D, D), D)
-        copy_of(buf.at[u, pl.ds(at, TOK), :], target.at[:, cols], sem.at[which]).start()
+        copy_of(x_ref.at[u, pl.ds(at, TOK), :], target.at[:, cols], sem.at[which]).start()
 
     for u in range(N_ULY):
         group = head_group(device_at(u))
-        loads[u].wait()
         for j in range(GROUP):
             store(u, j * TOK, dq_ref, group * GROUP + j, 0)
         store(u, GROUP * TOK, dk_ref, group, 1)
@@ -427,7 +448,7 @@
     pair_low = ((2,) + rows4, BF)
     head_low = ((N_ULY, h * TOK, D), BF)
     message = ((N_ULY, (GROUP + 2) * TOK, D), BF)
-    sems = pltpu.SemaphoreType.DMA((5,))
+    sems = pltpu.SemaphoreType.DMA((N_ULY,))
     dq0, local = call(
         functools.partial(local0_kernel, h),
         (order, (x0, vmem)),
@@ -444,34 +465,26 @@
         2 * h,
         "cross_first",
     )
-    dq1, cross_low = call(
+    d_scores, cross_low = call(
         functools.partial(cross1_kernel, h),
         (order, (x1, vmem), (kv_prev, vmem), (cross, hbm)),
-        ((head_sums, hbm), (pair_low, vmem)),
-        [
-            pltpu.VMEM(*head_sums),
-            pltpu.VMEM(*pair_sums),
-            pltpu.VMEM(*pair_sums),
-            sems,
-        ],
+        ((((2, HALF, h * HALF), BF), vmem), (pair_low, vmem)),
+        [pltpu.VMEM(*pair_sums), pltpu.VMEM(*pair_sums), sems],
         2 * h,
         "cross_last",
     )
     back = shift_slot(cross_low, -1)
     msg, local = call(
         functools.partial(local1_kernel, h, kv_at),
-        (order, (x1, vmem), (x0, vmem), (dq1, hbm), (local, hbm), (msg, hbm)),
+        (
+            order, (x1, vmem), (x0, vmem), (kv_prev, vmem), (d_scores, vmem), (local, hbm),
+            (msg, hbm),
+        ),
         ((message, hbm), (pair_sums, vmem)),
-        [
-            pltpu.VMEM(*head_sums),
-            pltpu.VMEM(*head_sums),
-            pltpu.VMEM(*pair_sums),
-            pltpu.VMEM(*head_low),
-            sems,
-        ],
+        [pltpu.VMEM(*head_sums), pltpu.VMEM(*pair_sums), pltpu.VMEM(*head_low), sems],
         3 * h,
         "local_last",
-        {5: 0},
+        {6: 0},
     )
     (msg,) = call(
         functools.partial(add_kernel, h),
@@ -485,15 +498,13 @@
     result = exchange(msg)
     return call(
         unpack_kernel,
-        ((result, hbm),),
+        ((result, vmem),),
         (
             (((TOK, N_ULY * GROUP * D), BF), hbm),
             (((TOK, N_ULY * D), BF), hbm),
             (((TOK, N_ULY * D), BF), hbm),
         ),
         [
-            pltpu.VMEM(*message),
-            pltpu.SemaphoreType.DMA((N_ULY,)),
             pltpu.SemaphoreType.DMA((3,)),
         ],
         0,

time: 94.8 us -> 91.5 us (0.965)
  Pallas kernels: 30.6 us -> 28.9 us
    pallas_call x8, Pallas kernels: 30.6 us -> 28.9 us  [call(): pl.pallas_call(kernel, in_specs=[pl.BlockSpec(memory_space=space) for _,...]
where the time goes in v4:
time: 91.5 us; the launch traced here: 91 us
  Pallas kernels  28.9 us (32%)
  blocking collectives  27.3 us (30%)
  waiting for transfers between devices  21.4 us (23%)
  starting transfers between devices  12.5 us (14%)
    pallas_call x8, Pallas kernels, call(): pl.pallas_call(kernel, in_specs=[pl.BlockSpec(memory_space=space) for _,...  28.9 us
    all_to_all x1, blocking collectives, exchange(): lax.all_to_all(value, ('blk', 'uly'), split_axis=0, concat_axis=0, axis_i...  27.3 us
    all_to_all x2, waiting for transfers between devices, exchange(): lax.all_to_all(value, ('blk', 'uly'), split_axis=0, concat_axis=0, axis_i...  16.9 us
    all_to_all x2, starting transfers between devices, exchange(): lax.all_to_all(value, ('blk', 'uly'), split_axis=0, concat_axis=0, axis_i...  10.6 us
    ppermute x2, waiting for transfers between devices, shift_slot(): return lax.ppermute(value, ('blk', 'uly'), pairs)  4.55 us
    ppermute x2, starting transfers between devices, shift_slot(): return lax.ppermute(value, ('blk', 'uly'), pairs)  1.9 us
  transfers between devices with their start and end apart: 4, of which 3 were waited for; matrix products, arithmetic and copies ran while one was open for 0% of the time, Pallas kernels for 21%

profile of v4, /device:TPU:64, one launch (start us, length us, event | category | flops | bytes accessed | tf_op | source)
XLA Modules:
  0.0 91.0 jit_solution(16556022975269455376)
XLA Ops:
  0.6 3.5 %pack_heads_0.1 = bf16[8,784,128]{2,1,0:T(8,128)(2,1)} custom-call(bf16[128,4096]{1,0:T(8,128)(2,1)} %refs_0_.3, bf16[128,4096]{1,0:T(8,128)(2,1)} %refs_1_.3, bf16[128,4096]{1,0:T(8,128)(2,1)} %refs_2_.3, f32[32,128]{1,0:T(8,128)} %bitcast.6, bf16[128,1024]{1,0:T(8,128)(2,1)} %refs_4_.1, bf16[128,1024]{1,0:T(8,128)(2,1)} %refs_5_.1), custom_call_target="tpu_custom_call" | custom-call | flops 671088640 | bytes 4194304 | tf_op jit(solution)/shard_map/pack_heads_0/pallas_call | solution.py:415
  4.1 5.5 %all-to-all-start = ((bf16[8,784,128]{2,1,0:T(8,128)(2,1)}), bf16[8,784,128]{2,1,0:T(8,128)(2,1)S(1)}, u32[]{:S(2)}, u32[]{:S(2)}) async-start(bf16[8,784,128]{2,1,0:T(8,128)(2,1)} %pack_heads_0.1), calls=%async_computation | async-start | bytes 3211264 | tf_op jit(solution)/shard_map/all_to_all | solution.py:403
  9.7 3.4 %pack_heads_2.1 = bf16[8,528,128]{2,1,0:T(8,128)(2,1)} custom-call(bf16[128,4096]{1,0:T(8,128)(2,1)} %refs_0_.3, bf16[128,4096]{1,0:T(8,128)(2,1)} %refs_1_.3, bf16[128,4096]{1,0:T(8,128)(2,1)} %refs_2_.3, f32[32,128]{1,0:T(8,128)} %bitcast.7), custom_call_target="tpu_custom_call" | custom-call | flops 671088640 | bytes 4194304 | tf_op jit(solution)/shard_map/pack_heads_2/pallas_call | solution.py:415
  13.1 0.0 copy-start
  13.1 16.9 %all-to-all-done.x_ref.x0_ref = bf16[8,784,128]{2,1,0:T(8,128)(2,1)S(1)} async-done(((bf16[8,784,128]{2,1,0:T(8,128)(2,1)}), bf16[8,784,128]{2,1,0:T(8,128)(2,1)S(1)}, u32[]{:S(2)}, u32[]{:S(2)}) %all-to-all-start) | async-done | bytes 1605664 | tf_op jit(solution)/shard_map/all_to_all | solution.py:403
  30.0 5.0 %all-to-all-start.1 = ((bf16[8,528,128]{2,1,0:T(8,128)(2,1)}), bf16[8,528,128]{2,1,0:T(8,128)(2,1)S(1)}, u32[]{:S(2)}, u32[]{:S(2)}) async-start(bf16[8,528,128]{2,1,0:T(8,128)(2,1)} %pack_heads_2.1), calls=%async_computation.1 | async-start | bytes 2162688 | tf_op jit(solution)/shard_map/all_to_all | solution.py:403
  35.0 1.6 %collective-permute-start = (bf16[8,256,128]{2,1,0:T(8,128)(2,1)S(1)}, bf16[8,256,128]{2,1,0:T(8,128)(2,1)S(1)}, u32[]{:S(2)}, u32[]{:S(2)}) collective-permute-start(bf16[8,256,128]{2,1,0:T(8,128)(2,1)S(1)} %slice.3), channel_id=1, source_target_pairs={{0,8},{1,9},{2,10},{3,11},{4,12},{5,13},{6,14},{7,15},{8,16},{9,17... | collective-permute-start | bytes 1572872 | tf_op jit(solution)/shard_map/ppermute | solution.py:398
  36.7 0.0 copy-done
  36.7 5.2 %local_first.1 = (f32[2,8,128,128]{3,2,1,0:T(8,128)S(1)}, f32[2,8,128,128]{3,2,1,0:T(8,128)}) custom-call(s32[2,16]{1,0:T(2,128)S(1)} %bitcast.2, bf16[8,784,128]{2,1,0:T(8,128)(2,1)S(1)} %all-to-all-done.x_ref.x0_ref), custom_call_target="tpu_custom_call" | custom-call | flops 4026531840 | bytes 4194304 | tf_op jit(solution)/shard_map/local_first/pallas_call | solution.py:415
  41.9 3.9 %collective-permute-done.kp_ref = bf16[8,256,128]{2,1,0:T(8,128)(2,1)S(1)} collective-permute-done((bf16[8,256,128]{2,1,0:T(8,128)(2,1)S(1)}, bf16[8,256,128]{2,1,0:T(8,128)(2,1)S(1)}, u32[]{:S(2)}, u32[]{:S(2)}) %collective-permute-start) | collective-permute-done | bytes 524320 | tf_op jit(solution)/shard_map/ppermute | solution.py:398
  45.8 4.7 %cross_first.1 = (bf16[8,768,128]{2,1,0:T(8,128)(2,1)}, f32[2,8,128,128]{3,2,1,0:T(8,128)}) custom-call(s32[2,16]{1,0:T(2,128)S(1)} %bitcast.3, bf16[8,784,128]{2,1,0:T(8,128)(2,1)S(1)} %all-to-all-done.x_ref.x0_ref, bf16[8,256,128]{2,1,0:T(8,128)(2,1)S(1)} %collective-permute-done.kp_ref, f32[2,8,128,128]{3,2,1,0:T(8,128)S(1)} %get-tuple-element.15.dq_in), custom_call_target="tpu_custom_call" | custom-call | flops 2684354560 | bytes 4194304 | tf_op jit(solution)/shard_map/cross_first/pallas_call | solution.py:415
  50.5 0.0 all-to-all-done.1.x_ref
  50.5 4.1 %cross_last.1 = (bf16[2,512,1024]{2,1,0:T(8,128)(2,1)S(1)}, bf16[2,8,128,128]{3,2,1,0:T(8,128)(2,1)S(1)}) custom-call(s32[2,16]{1,0:T(2,128)S(1)} %bitcast.4, bf16[8,528,128]{2,1,0:T(8,128)(2,1)S(1)} %all-to-all-done.1.x_ref, bf16[8,256,128]{2,1,0:T(8,128)(2,1)S(1)} %collective-permute-done.kp_ref, f32[2,8,128,128]{3,2,1,0:T(8,128)} %get-tuple-element.16.cross_hbm), custom_call_target="tpu_custom_call" | custom-call | flops 2684354560 | bytes 4194304 | tf_op jit(solution)/shard_map/cross_last/pallas_call | solution.py:415
  54.6 0.3 collective-permute-start.1
  54.9 6.1 %local_last.1 = (bf16[8,768,128]{2,1,0:T(8,128)(2,1)}, f32[2,8,128,128]{3,2,1,0:T(8,128)S(1)}) custom-call(s32[2,16]{1,0:T(2,128)S(1)} %bitcast.5, bf16[8,528,128]{2,1,0:T(8,128)(2,1)S(1)} %all-to-all-done.1.x_ref, bf16[8,784,128]{2,1,0:T(8,128)(2,1)S(1)} %all-to-all-done.x_ref.x0_ref, ...), custom_call_target="tpu_custom_call", output_to_operand_aliasing={{0}: (6, {})} | custom-call | flops 4026531840 | bytes 4194304 | tf_op jit(solution)/shard_map/local_last/pallas_call | solution.py:415
  60.9 0.6 collective-permute-done.1.back_ref
  61.6 0.9 add_returned.1
  62.5 27.3 %all_to_all.15.x_ref = bf16[8,768,128]{2,1,0:T(8,128)(2,1)S(1)} all-to-all(bf16[8,768,128]{2,1,0:T(8,128)(2,1)} %add_returned.1), channel_id=1, replica_groups={{0,2,4,6,1,3,5,7},{15,14,13,12,11,10,9,8},{16,18,20,22,17,19,21,23},{31..., dimensions={0} | all-to-all | bytes 3145728 | tf_op jit(solution)/shard_map/all_to_all | solution.py:403
  89.7 1.1 %unpack.1 = (bf16[128,4096]{1,0:T(8,128)(2,1)}, bf16[128,1024]{1,0:T(8,128)(2,1)}, bf16[128,1024]{1,0:T(8,128)(2,1)}) custom-call(bf16[8,768,128]{2,1,0:T(8,128)(2,1)S(1)} %all_to_all.15.x_ref), custom_call_target="tpu_custom_call" | custom-call | bytes 4194304 | tf_op jit(solution)/shard_map/unpack/pallas_call | solution.py:415
  (1 shorter events, 0.0 us)
Async XLA Ops:
  4.1 25.9 %all-to-all-start = ((bf16[8,784,128]{2,1,0:T(8,128)(2,1)}), bf16[8,784,128]{2,1,0:T(8,128)(2,1)S(1)}, u32[]{:S(2)}, u32[]{:S(2)}) async-start(bf16[8,784,128]{2,1,0:T(8,128)(2,1)} %pack_heads_0.1), calls=%async_computation | async-start | bytes 3211264 | tf_op jit(solution)/shard_map/all_to_all | solution.py:403
  13.1 23.6 %copy-start = (s32[16,2]{0,1:T(2,128)S(1)}, s32[16,2]{0,1:T(2,128)}, u32[]{:S(2)}) copy-start(s32[16,2]{0,1:T(2,128)} %param.13) | copy-start | bytes 388
  30.0 20.5 %all-to-all-start.1 = ((bf16[8,528,128]{2,1,0:T(8,128)(2,1)}), bf16[8,528,128]{2,1,0:T(8,128)(2,1)S(1)}, u32[]{:S(2)}, u32[]{:S(2)}) async-start(bf16[8,528,128]{2,1,0:T(8,128)(2,1)} %pack_heads_2.1), calls=%async_computation.1 | async-start | bytes 2162688 | tf_op jit(solution)/shard_map/all_to_all | solution.py:403
  35.0 10.8 %collective-permute-start = (bf16[8,256,128]{2,1,0:T(8,128)(2,1)S(1)}, bf16[8,256,128]{2,1,0:T(8,128)(2,1)S(1)}, u32[]{:S(2)}, u32[]{:S(2)}) collective-permute-start(bf16[8,256,128]{2,1,0:T(8,128)(2,1)S(1)} %slice.3), channel_id=1, source_target_pairs={{0,8},{1,9},{2,10},{3,11},{4,12},{5,13},{6,14},{7,15},{8,16},{9,17... | collective-permute-start | bytes 1572872 | tf_op jit(solution)/shard_map/ppermute | solution.py:398
  54.6 7.0 %collective-permute-start.1 = (bf16[2,8,128,128]{3,2,1,0:T(8,128)(2,1)S(1)}, bf16[2,8,128,128]{3,2,1,0:T(8,128)(2,1)S(1)}, u32[]{:S(2)}, u32[]{:S(2)}) collective-permute-start(bf16[2,8,128,128]{3,2,1,0:T(8,128)(2,1)S(1)} %get-tuple-element.21), channel_id=1, source_target_pairs={{0,121},{1,120},{2,123},{3,122},{4,125},{5,124},{6,127},{7,126},{8... | collective-permute-start | bytes 1572872 | tf_op jit(solution)/shard_map/ppermute | solution.py:398

commit v5 on v4

--- a/solution.py
+++ b/solution.py
@@ -19,7 +19,7 @@
 BF = jnp.bfloat16
 F32 = jnp.float32
 MIB = 1 << 20
-ORDERS = ((0, 2, 4, 6, 1, 3, 5, 7), (7, 6, 5, 4, 3, 2, 1, 0))
+ORDERS = ((0, 2, 4, 6, 1, 3, 5, 7), (7, 4, 3, 0, 6, 5, 2, 1))
 PLACES = tuple(tuple(order.index(u) for u in range(N_ULY)) for order in ORDERS)
 
 
@@ -421,9 +421,9 @@
         input_output_aliases=aliases or {},
         compiler_params=params(),
         cost_estimate=pl.CostEstimate(
-            flops=units * 5 * 2 * 512 * 512 * 128 * 2,
-            bytes_accessed=4 * MIB,
-            transcendentals=units * 512 * 512,
+            flops=int(units * 5 * 2 * 512 * 512 * 128 * 2),
+            bytes_accessed=int(min(units, 4) * MIB),
+            transcendentals=int(units * 512 * 512),
         ),
         name=name,
     )(*[placed(array, space) for array, space in inputs])

time: 91.5 us -> 90.8 us (level)
  starting transfers between devices: 12.5 us -> 10.1 us
  waiting for transfers between devices: 21.4 us -> 23.2 us
    all_to_all x2, starting transfers between devices: 10.6 us -> 9.1 us  [exchange(): lax.all_to_all(value, ('blk', 'uly'), split_axis=0, concat_axis=0, axis_i...]
where the time goes in v5:
time: 90.8 us; the launch traced here: 90.4 us
  Pallas kernels  28.9 us (32%)
  blocking collectives  27.3 us (30%)
  waiting for transfers between devices  23.2 us (26%)
  starting transfers between devices  10.1 us (11%)
    pallas_call x8, Pallas kernels, call(): pl.pallas_call(kernel, in_specs=[pl.BlockSpec(memory_space=space) for _,...  28.9 us
    all_to_all x1, blocking collectives, exchange(): lax.all_to_all(value, ('blk', 'uly'), split_axis=0, concat_axis=0, axis_i...  27.3 us
    all_to_all x2, waiting for transfers between devices, exchange(): lax.all_to_all(value, ('blk', 'uly'), split_axis=0, concat_axis=0, axis_i...  17.7 us
    all_to_all x2, starting transfers between devices, exchange(): lax.all_to_all(value, ('blk', 'uly'), split_axis=0, concat_axis=0, axis_i...  9.1 us
    ppermute x2, waiting for transfers between devices, shift_slot(): return lax.ppermute(value, ('blk', 'uly'), pairs)  5.43 us
  transfers between devices with their start and end apart: 4, of which 3 were waited for; matrix products, arithmetic and copies ran while one was open for 0% of the time, Pallas kernels for 21%

profile of v5, /device:TPU:64, one launch (start us, length us, event | category | flops | bytes accessed | tf_op | source)
XLA Modules:
  0.0 90.4 jit_solution(12783462366351184886)
XLA Ops:
  0.6 3.5 %pack_heads_0.1 = bf16[8,784,128]{2,1,0:T(8,128)(2,1)} custom-call(bf16[128,4096]{1,0:T(8,128)(2,1)} %refs_0_.3, bf16[128,4096]{1,0:T(8,128)(2,1)} %refs_1_.3, bf16[128,4096]{1,0:T(8,128)(2,1)} %refs_2_.3, f32[32,128]{1,0:T(8,128)} %bitcast.6, bf16[128,1024]{1,0:T(8,128)(2,1)} %refs_4_.1, bf16[128,1024]{1,0:T(8,128)(2,1)} %refs_5_.1), custom_call_target="tpu_custom_call" | custom-call | flops 671088640 | bytes 1048576 | tf_op jit(solution)/shard_map/pack_heads_0/pallas_call | solution.py:415
  4.1 5.5 %all-to-all-start = ((bf16[8,784,128]{2,1,0:T(8,128)(2,1)}), bf16[8,784,128]{2,1,0:T(8,128)(2,1)S(1)}, u32[]{:S(2)}, u32[]{:S(2)}) async-start(bf16[8,784,128]{2,1,0:T(8,128)(2,1)} %pack_heads_0.1), calls=%async_computation | async-start | bytes 3211264 | tf_op jit(solution)/shard_map/all_to_all | solution.py:403
  9.7 3.4 %pack_heads_2.1 = bf16[8,528,128]{2,1,0:T(8,128)(2,1)} custom-call(bf16[128,4096]{1,0:T(8,128)(2,1)} %refs_0_.3, bf16[128,4096]{1,0:T(8,128)(2,1)} %refs_1_.3, bf16[128,4096]{1,0:T(8,128)(2,1)} %refs_2_.3, f32[32,128]{1,0:T(8,128)} %bitcast.7), custom_call_target="tpu_custom_call" | custom-call | flops 671088640 | bytes 1048576 | tf_op jit(solution)/shard_map/pack_heads_2/pallas_call | solution.py:415
  13.1 0.0 copy-start
  13.1 17.7 %all-to-all-done.x_ref.x0_ref = bf16[8,784,128]{2,1,0:T(8,128)(2,1)S(1)} async-done(((bf16[8,784,128]{2,1,0:T(8,128)(2,1)}), bf16[8,784,128]{2,1,0:T(8,128)(2,1)S(1)}, u32[]{:S(2)}, u32[]{:S(2)}) %all-to-all-start) | async-done | bytes 1605664 | tf_op jit(solution)/shard_map/all_to_all | solution.py:403
  30.8 3.6 %all-to-all-start.1 = ((bf16[8,528,128]{2,1,0:T(8,128)(2,1)}), bf16[8,528,128]{2,1,0:T(8,128)(2,1)S(1)}, u32[]{:S(2)}, u32[]{:S(2)}) async-start(bf16[8,528,128]{2,1,0:T(8,128)(2,1)} %pack_heads_2.1), calls=%async_computation.1 | async-start | bytes 2162688 | tf_op jit(solution)/shard_map/all_to_all | solution.py:403
  34.4 0.8 collective-permute-start
  35.2 0.0 copy-done
  35.2 5.2 %local_first.1 = (f32[2,8,128,128]{3,2,1,0:T(8,128)S(1)}, f32[2,8,128,128]{3,2,1,0:T(8,128)}) custom-call(s32[2,16]{1,0:T(2,128)S(1)} %bitcast.2, bf16[8,784,128]{2,1,0:T(8,128)(2,1)S(1)} %all-to-all-done.x_ref.x0_ref), custom_call_target="tpu_custom_call" | custom-call | flops 4026531840 | bytes 4194304 | tf_op jit(solution)/shard_map/local_first/pallas_call | solution.py:415
  40.4 4.8 %collective-permute-done.kp_ref = bf16[8,256,128]{2,1,0:T(8,128)(2,1)S(1)} collective-permute-done((bf16[8,256,128]{2,1,0:T(8,128)(2,1)S(1)}, bf16[8,256,128]{2,1,0:T(8,128)(2,1)S(1)}, u32[]{:S(2)}, u32[]{:S(2)}) %collective-permute-start) | collective-permute-done | bytes 524320 | tf_op jit(solution)/shard_map/ppermute | solution.py:398
  45.2 4.7 %cross_first.1 = (bf16[8,768,128]{2,1,0:T(8,128)(2,1)}, f32[2,8,128,128]{3,2,1,0:T(8,128)}) custom-call(s32[2,16]{1,0:T(2,128)S(1)} %bitcast.3, bf16[8,784,128]{2,1,0:T(8,128)(2,1)S(1)} %all-to-all-done.x_ref.x0_ref, bf16[8,256,128]{2,1,0:T(8,128)(2,1)S(1)} %collective-permute-done.kp_ref, f32[2,8,128,128]{3,2,1,0:T(8,128)S(1)} %get-tuple-element.15.dq_in), custom_call_target="tpu_custom_call" | custom-call | flops 2684354560 | bytes 4194304 | tf_op jit(solution)/shard_map/cross_first/pallas_call | solution.py:415
  49.9 0.0 all-to-all-done.1.x_ref
  49.9 4.1 %cross_last.1 = (bf16[2,512,1024]{2,1,0:T(8,128)(2,1)S(1)}, bf16[2,8,128,128]{3,2,1,0:T(8,128)(2,1)S(1)}) custom-call(s32[2,16]{1,0:T(2,128)S(1)} %bitcast.4, bf16[8,528,128]{2,1,0:T(8,128)(2,1)S(1)} %all-to-all-done.1.x_ref, bf16[8,256,128]{2,1,0:T(8,128)(2,1)S(1)} %collective-permute-done.kp_ref, f32[2,8,128,128]{3,2,1,0:T(8,128)} %get-tuple-element.16.cross_hbm), custom_call_target="tpu_custom_call" | custom-call | flops 2684354560 | bytes 4194304 | tf_op jit(solution)/shard_map/cross_last/pallas_call | solution.py:415
  54.0 0.3 collective-permute-start.1
  54.2 6.1 %local_last.1 = (bf16[8,768,128]{2,1,0:T(8,128)(2,1)}, f32[2,8,128,128]{3,2,1,0:T(8,128)S(1)}) custom-call(s32[2,16]{1,0:T(2,128)S(1)} %bitcast.5, bf16[8,528,128]{2,1,0:T(8,128)(2,1)S(1)} %all-to-all-done.1.x_ref, bf16[8,784,128]{2,1,0:T(8,128)(2,1)S(1)} %all-to-all-done.x_ref.x0_ref, ...), custom_call_target="tpu_custom_call", output_to_operand_aliasing={{0}: (6, {})} | custom-call | flops 4026531840 | bytes 4194304 | tf_op jit(solution)/shard_map/local_last/pallas_call | solution.py:415
  60.3 0.6 collective-permute-done.1.back_ref
  60.9 0.9 add_returned.1
  61.8 27.3 %all_to_all.15.x_ref = bf16[8,768,128]{2,1,0:T(8,128)(2,1)S(1)} all-to-all(bf16[8,768,128]{2,1,0:T(8,128)(2,1)} %add_returned.1), channel_id=1, replica_groups={{0,2,4,6,1,3,5,7},{15,12,11,8,14,13,10,9},{16,18,20,22,17,19,21,23},{31..., dimensions={0} | all-to-all | bytes 3145728 | tf_op jit(solution)/shard_map/all_to_all | solution.py:403
  89.1 1.1 %unpack.1 = (bf16[128,4096]{1,0:T(8,128)(2,1)}, bf16[128,1024]{1,0:T(8,128)(2,1)}, bf16[128,1024]{1,0:T(8,128)(2,1)}) custom-call(bf16[8,768,128]{2,1,0:T(8,128)(2,1)S(1)} %all_to_all.15.x_ref), custom_call_target="tpu_custom_call" | custom-call | tf_op jit(solution)/shard_map/unpack/pallas_call | solution.py:415
  (1 shorter events, 0.0 us)
Async XLA Ops:
  4.1 26.7 %all-to-all-start = ((bf16[8,784,128]{2,1,0:T(8,128)(2,1)}), bf16[8,784,128]{2,1,0:T(8,128)(2,1)S(1)}, u32[]{:S(2)}, u32[]{:S(2)}) async-start(bf16[8,784,128]{2,1,0:T(8,128)(2,1)} %pack_heads_0.1), calls=%async_computation | async-start | bytes 3211264 | tf_op jit(solution)/shard_map/all_to_all | solution.py:403
  13.1 22.1 %copy-start = (s32[16,2]{0,1:T(2,128)S(1)}, s32[16,2]{0,1:T(2,128)}, u32[]{:S(2)}) copy-start(s32[16,2]{0,1:T(2,128)} %param.13) | copy-start | bytes 388
  30.8 19.1 %all-to-all-start.1 = ((bf16[8,528,128]{2,1,0:T(8,128)(2,1)}), bf16[8,528,128]{2,1,0:T(8,128)(2,1)S(1)}, u32[]{:S(2)}, u32[]{:S(2)}) async-start(bf16[8,528,128]{2,1,0:T(8,128)(2,1)} %pack_heads_2.1), calls=%async_computation.1 | async-start | bytes 2162688 | tf_op jit(solution)/shard_map/all_to_all | solution.py:403
  34.4 10.8 %collective-permute-start = (bf16[8,256,128]{2,1,0:T(8,128)(2,1)S(1)}, bf16[8,256,128]{2,1,0:T(8,128)(2,1)S(1)}, u32[]{:S(2)}, u32[]{:S(2)}) collective-permute-start(bf16[8,256,128]{2,1,0:T(8,128)(2,1)S(1)} %slice.3), channel_id=1, source_target_pairs={{0,8},{1,9},{2,10},{3,11},{4,12},{5,13},{6,14},{7,15},{8,16},{9,17... | collective-permute-start | bytes 1572872 | tf_op jit(solution)/shard_map/ppermute | solution.py:398
  54.0 7.0 %collective-permute-start.1 = (bf16[2,8,128,128]{3,2,1,0:T(8,128)(2,1)S(1)}, bf16[2,8,128,128]{3,2,1,0:T(8,128)(2,1)S(1)}, u32[]{:S(2)}, u32[]{:S(2)}) collective-permute-start(bf16[2,8,128,128]{3,2,1,0:T(8,128)(2,1)S(1)} %get-tuple-element.21), channel_id=1, source_target_pairs={{0,121},{1,120},{2,123},{3,122},{4,125},{5,124},{6,127},{7,126},{8... | collective-permute-start | bytes 1572872 | tf_op jit(solution)/shard_map/ppermute | solution.py:398

commit v6 on v5

--- a/solution.py
+++ b/solution.py
@@ -90,6 +90,7 @@
     for u in range(N_ULY):
         loaded = buf.at[u, pl.ds(0, rows), :]
         copy_of(loaded, loaded, sem.at[0, u]).wait()
+        copy_of(loaded, msg_ref.at[u, pl.ds(0, rows), :], sem.at[2, u]).start()
         copy_of(o_buf.at[u], o_buf.at[u], sem.at[1, u]).wait()
         at = groups[u] * GROUP + first
         stats = jnp.zeros((8, TOK), F32)
@@ -108,9 +109,13 @@
         p2 = stats - p0 - p1
         pieces = jnp.concatenate([p0, p1, p2, jnp.zeros_like(p0)], axis=0)
         buf[u, rows : rows + STAT, :] = pieces.astype(BF)
-        copy_of(buf.at[u], msg_ref.at[u], sem.at[2, u]).start()
+    numbers = pl.ds(rows, STAT)
+    last = copy_of(buf.at[:, numbers, :], msg_ref.at[:, numbers, :], sem.at[3, 1])
+    last.start()
     for u in range(N_ULY):
-        copy_of(buf.at[u], msg_ref.at[u], sem.at[2, u]).wait()
+        loaded = buf.at[u, pl.ds(0, rows), :]
+        copy_of(loaded, msg_ref.at[u, pl.ds(0, rows), :], sem.at[2, u]).wait()
+    last.wait()
 
 
 def pack(queries, grads, outputs, lse, kv, first, heads):
@@ -370,6 +375,12 @@
         send.wait()
 
 
+def take_kernel(at, x_ref, out_ref, sem):
+    copy = copy_of(x_ref.at[:, pl.ds(at, out_ref.shape[1]), :], out_ref, sem)
+    copy.start()
+    copy.wait()
+
+
 def unpack_kernel(x_ref, dq_ref, dk_ref, dv_ref, sem):
     def store(u, at, target, column, which):
         cols = pl.ds(pl.multiple_of(column * D, D), D)
@@ -440,7 +451,15 @@
     msg1 = pack(queries, output_gradient, outputs, lse, (), h, h)
     x0, msg1 = lax.optimization_barrier((x0, msg1))
     x1 = exchange(msg1)
-    kv_prev = shift_slot(x0[:, kv_at : kv_at + 2 * TOK, :], 1)
+    (keys,) = call(
+        functools.partial(take_kernel, kv_at),
+        ((x0, pltpu.VMEM),),
+        ((((N_ULY, 2 * TOK, D), BF), pltpu.VMEM),),
+        [pltpu.SemaphoreType.DMA],
+        0,
+        "take_keys",
+    )
+    kv_prev = shift_slot(keys, 1)
 
     vmem, hbm = pltpu.VMEM, pltpu.HBM
     head_sums = ((h,) + rows4, F32)

time: 90.8 us -> 90.8 us (level)
    pallas_call x8 -> x9, Pallas kernels: 28.9 us -> 28.7 us  [call(): pl.pallas_call(kernel, in_specs=[pl.BlockSpec(memory_space=space) for _,...]
where the time goes in v6:
time: 90.8 us; the launch traced here: 90.3 us
  Pallas kernels  28.7 us (32%)
  blocking collectives  27.2 us (30%)
  waiting for transfers between devices  23.3 us (26%)
  starting transfers between devices  10.1 us (11%)
    pallas_call x9, Pallas kernels, call(): pl.pallas_call(kernel, in_specs=[pl.BlockSpec(memory_space=space) for _,...  28.7 us
    all_to_all x1, blocking collectives, exchange(): lax.all_to_all(value, ('blk', 'uly'), split_axis=0, concat_axis=0, axis_i...  27.2 us
    all_to_all x2, waiting for transfers between devices, exchange(): lax.all_to_all(value, ('blk', 'uly'), split_axis=0, concat_axis=0, axis_i...  17.8 us
    all_to_all x2, starting transfers between devices, exchange(): lax.all_to_all(value, ('blk', 'uly'), split_axis=0, concat_axis=0, axis_i...  9.1 us
    ppermute x2, waiting for transfers between devices, shift_slot(): return lax.ppermute(value, ('blk', 'uly'), pairs)  5.47 us
  transfers between devices with their start and end apart: 4, of which 3 were waited for; matrix products, arithmetic and copies ran while one was open for 0% of the time, Pallas kernels for 21%

profile of v6, /device:TPU:64, one launch (start us, length us, event | category | flops | bytes accessed | tf_op | source)
XLA Modules:
  0.0 90.3 jit_solution(8545620211962782711)
XLA Ops:
  0.6 3.4 %pack_heads_0.1 = bf16[8,784,128]{2,1,0:T(8,128)(2,1)} custom-call(bf16[128,4096]{1,0:T(8,128)(2,1)} %refs_0_.3, bf16[128,4096]{1,0:T(8,128)(2,1)} %refs_1_.3, bf16[128,4096]{1,0:T(8,128)(2,1)} %refs_2_.3, f32[32,128]{1,0:T(8,128)} %bitcast.6, bf16[128,1024]{1,0:T(8,128)(2,1)} %refs_4_.1, bf16[128,1024]{1,0:T(8,128)(2,1)} %refs_5_.1), custom_call_target="tpu_custom_call" | custom-call | flops 671088640 | bytes 1048576 | tf_op jit(solution)/shard_map/pack_heads_0/pallas_call | solution.py:426
  4.0 5.5 %all-to-all-start = ((bf16[8,784,128]{2,1,0:T(8,128)(2,1)}), bf16[8,784,128]{2,1,0:T(8,128)(2,1)S(1)}, u32[]{:S(2)}, u32[]{:S(2)}) async-start(bf16[8,784,128]{2,1,0:T(8,128)(2,1)} %pack_heads_0.1), calls=%async_computation | async-start | bytes 3211264 | tf_op jit(solution)/shard_map/all_to_all | solution.py:414
  9.6 3.4 %pack_heads_2.1 = bf16[8,528,128]{2,1,0:T(8,128)(2,1)} custom-call(bf16[128,4096]{1,0:T(8,128)(2,1)} %refs_0_.3, bf16[128,4096]{1,0:T(8,128)(2,1)} %refs_1_.3, bf16[128,4096]{1,0:T(8,128)(2,1)} %refs_2_.3, f32[32,128]{1,0:T(8,128)} %bitcast.7), custom_call_target="tpu_custom_call" | custom-call | flops 671088640 | bytes 1048576 | tf_op jit(solution)/shard_map/pack_heads_2/pallas_call | solution.py:426
  13.0 17.8 %all-to-all-done.x_ref.x0_ref = bf16[8,784,128]{2,1,0:T(8,128)(2,1)S(1)} async-done(((bf16[8,784,128]{2,1,0:T(8,128)(2,1)}), bf16[8,784,128]{2,1,0:T(8,128)(2,1)S(1)}, u32[]{:S(2)}, u32[]{:S(2)}) %all-to-all-start) | async-done | bytes 1605664 | tf_op jit(solution)/shard_map/all_to_all | solution.py:414
  30.8 3.6 %all-to-all-start.1 = ((bf16[8,528,128]{2,1,0:T(8,128)(2,1)}), bf16[8,528,128]{2,1,0:T(8,128)(2,1)S(1)}, u32[]{:S(2)}, u32[]{:S(2)}) async-start(bf16[8,528,128]{2,1,0:T(8,128)(2,1)} %pack_heads_2.1), calls=%async_computation.1 | async-start | bytes 2162688 | tf_op jit(solution)/shard_map/all_to_all | solution.py:414
  34.3 0.0 copy-start
  34.4 0.8 collective-permute-start
  35.2 0.0 copy-done
  35.2 5.2 %local_first.1 = (f32[2,8,128,128]{3,2,1,0:T(8,128)S(1)}, f32[2,8,128,128]{3,2,1,0:T(8,128)}) custom-call(s32[2,16]{1,0:T(2,128)S(1)} %bitcast.2, bf16[8,784,128]{2,1,0:T(8,128)(2,1)S(1)} %all-to-all-done.x_ref.x0_ref), custom_call_target="tpu_custom_call" | custom-call | flops 4026531840 | bytes 4194304 | tf_op jit(solution)/shard_map/local_first/pallas_call | solution.py:426
  40.4 4.8 %collective-permute-done.kp_ref = bf16[8,256,128]{2,1,0:T(8,128)(2,1)S(1)} collective-permute-done((bf16[8,256,128]{2,1,0:T(8,128)(2,1)S(1)}, bf16[8,256,128]{2,1,0:T(8,128)(2,1)S(1)}, u32[]{:S(2)}, u32[]{:S(2)}) %collective-permute-start) | collective-permute-done | bytes 524320 | tf_op jit(solution)/shard_map/ppermute | solution.py:409
  45.2 4.7 %cross_first.1 = (bf16[8,768,128]{2,1,0:T(8,128)(2,1)}, f32[2,8,128,128]{3,2,1,0:T(8,128)}) custom-call(s32[2,16]{1,0:T(2,128)S(1)} %bitcast.3, bf16[8,784,128]{2,1,0:T(8,128)(2,1)S(1)} %all-to-all-done.x_ref.x0_ref, bf16[8,256,128]{2,1,0:T(8,128)(2,1)S(1)} %collective-permute-done.kp_ref, f32[2,8,128,128]{3,2,1,0:T(8,128)S(1)} %get-tuple-element.15.dq_in), custom_call_target="tpu_custom_call" | custom-call | flops 2684354560 | bytes 4194304 | tf_op jit(solution)/shard_map/cross_first/pallas_call | solution.py:426
  49.9 0.0 all-to-all-done.1.x_ref
  49.9 4.0 %cross_last.1 = (bf16[2,512,1024]{2,1,0:T(8,128)(2,1)S(1)}, bf16[2,8,128,128]{3,2,1,0:T(8,128)(2,1)S(1)}) custom-call(s32[2,16]{1,0:T(2,128)S(1)} %bitcast.4, bf16[8,528,128]{2,1,0:T(8,128)(2,1)S(1)} %all-to-all-done.1.x_ref, bf16[8,256,128]{2,1,0:T(8,128)(2,1)S(1)} %collective-permute-done.kp_ref, f32[2,8,128,128]{3,2,1,0:T(8,128)} %get-tuple-element.16.cross_hbm), custom_call_target="tpu_custom_call" | custom-call | flops 2684354560 | bytes 4194304 | tf_op jit(solution)/shard_map/cross_last/pallas_call | solution.py:426
  53.9 0.3 collective-permute-start.1
  54.2 6.0 %local_last.1 = (bf16[8,768,128]{2,1,0:T(8,128)(2,1)}, f32[2,8,128,128]{3,2,1,0:T(8,128)S(1)}) custom-call(s32[2,16]{1,0:T(2,128)S(1)} %bitcast.5, bf16[8,528,128]{2,1,0:T(8,128)(2,1)S(1)} %all-to-all-done.1.x_ref, bf16[8,784,128]{2,1,0:T(8,128)(2,1)S(1)} %all-to-all-done.x_ref.x0_ref, ...), custom_call_target="tpu_custom_call", output_to_operand_aliasing={{0}: (6, {})} | custom-call | flops 4026531840 | bytes 4194304 | tf_op jit(solution)/shard_map/local_last/pallas_call | solution.py:426
  60.2 0.7 collective-permute-done.1.back_ref
  60.9 0.9 add_returned.1
  61.7 27.2 %all_to_all.15.x_ref = bf16[8,768,128]{2,1,0:T(8,128)(2,1)S(1)} all-to-all(bf16[8,768,128]{2,1,0:T(8,128)(2,1)} %add_returned.1), channel_id=1, replica_groups={{0,2,4,6,1,3,5,7},{15,12,11,8,14,13,10,9},{16,18,20,22,17,19,21,23},{31..., dimensions={0} | all-to-all | bytes 3145728 | tf_op jit(solution)/shard_map/all_to_all | solution.py:414
  89.0 1.1 %unpack.1 = (bf16[128,4096]{1,0:T(8,128)(2,1)}, bf16[128,1024]{1,0:T(8,128)(2,1)}, bf16[128,1024]{1,0:T(8,128)(2,1)}) custom-call(bf16[8,768,128]{2,1,0:T(8,128)(2,1)S(1)} %all_to_all.15.x_ref), custom_call_target="tpu_custom_call" | custom-call | tf_op jit(solution)/shard_map/unpack/pallas_call | solution.py:426
  (1 shorter events, 0.0 us)
Async XLA Ops:
  4.0 26.7 %all-to-all-start = ((bf16[8,784,128]{2,1,0:T(8,128)(2,1)}), bf16[8,784,128]{2,1,0:T(8,128)(2,1)S(1)}, u32[]{:S(2)}, u32[]{:S(2)}) async-start(bf16[8,784,128]{2,1,0:T(8,128)(2,1)} %pack_heads_0.1), calls=%async_computation | async-start | bytes 3211264 | tf_op jit(solution)/shard_map/all_to_all | solution.py:414
  30.8 19.1 %all-to-all-start.1 = ((bf16[8,528,128]{2,1,0:T(8,128)(2,1)}), bf16[8,528,128]{2,1,0:T(8,128)(2,1)S(1)}, u32[]{:S(2)}, u32[]{:S(2)}) async-start(bf16[8,528,128]{2,1,0:T(8,128)(2,1)} %pack_heads_2.1), calls=%async_computation.1 | async-start | bytes 2162688 | tf_op jit(solution)/shard_map/all_to_all | solution.py:414
  34.3 0.8 copy-start
  34.4 10.8 %collective-permute-start = (bf16[8,256,128]{2,1,0:T(8,128)(2,1)S(1)}, bf16[8,256,128]{2,1,0:T(8,128)(2,1)S(1)}, u32[]{:S(2)}, u32[]{:S(2)}) collective-permute-start(bf16[8,256,128]{2,1,0:T(8,128)(2,1)S(1)} %take_keys.1), channel_id=1, source_target_pairs={{0,8},{1,9},{2,10},{3,11},{4,12},{5,13},{6,14},{7,15},{8,16},{9,17... | collective-permute-start | bytes 1572872 | tf_op jit(solution)/shard_map/ppermute | solution.py:409
  53.9 7.0 %collective-permute-start.1 = (bf16[2,8,128,128]{3,2,1,0:T(8,128)(2,1)S(1)}, bf16[2,8,128,128]{3,2,1,0:T(8,128)(2,1)S(1)}, u32[]{:S(2)}, u32[]{:S(2)}) collective-permute-start(bf16[2,8,128,128]{3,2,1,0:T(8,128)(2,1)S(1)} %get-tuple-element.21), channel_id=1, source_target_pairs={{0,121},{1,120},{2,123},{3,122},{4,125},{5,124},{6,127},{7,126},{8... | collective-permute-start | bytes 1572872 | tf_op jit(solution)/shard_map/ppermute | solution.py:409

commit v7 on v6

--- a/solution.py
+++ b/solution.py
@@ -314,11 +314,17 @@
     cross_tiles(low, prev_low, lower_sees, x_ref, stats, heads, kp_ref, dkv, first, second)
     store = copy_of(dkv, cross_hbm, sem.at[0])
     store.start()
+    sends = []
     for j in range(heads):
+        rows = pl.ds(j * TOK, TOK)
         out[:, j * TOK : (j + 1) * TOK, :] = (dq[j] + dq_in[j]).astype(BF)
-    send = send_rows(out, msg_hbm, 0, sem.at[1])
+        for u in range(N_ULY):
+            target = msg_hbm.at[place_of(u), rows, :]
+            copy_of(out.at[u, rows, :], target, sem.at[1 + j]).start()
+        sends.append(copy_of(out.at[:, rows, :], out.at[:, rows, :], sem.at[1 + j]))
     store.wait()
-    send.wait()
+    for send in sends:
+        send.wait()
 
 
 def cross1_kernel(heads, order_ref, x_ref, kp_ref, cross_hbm, ds_out, cross_out, dkv, held, sem):

time: 90.8 us -> 90.7 us (level)
  no operation moved by 1% of the time
where the time goes in v7:
time: 90.7 us; the launch traced here: 90.2 us
  Pallas kernels  28.7 us (32%)
  blocking collectives  27.2 us (30%)
  waiting for transfers between devices  23.3 us (26%)
  starting transfers between devices  10.1 us (11%)
    pallas_call x9, Pallas kernels, call(): pl.pallas_call(kernel, in_specs=[pl.BlockSpec(memory_space=space) for _,...  28.7 us
    all_to_all x1, blocking collectives, exchange(): lax.all_to_all(value, ('blk', 'uly'), split_axis=0, concat_axis=0, axis_i...  27.2 us
    all_to_all x2, waiting for transfers between devices, exchange(): lax.all_to_all(value, ('blk', 'uly'), split_axis=0, concat_axis=0, axis_i...  17.8 us
    all_to_all x2, starting transfers between devices, exchange(): lax.all_to_all(value, ('blk', 'uly'), split_axis=0, concat_axis=0, axis_i...  9.1 us
    ppermute x2, waiting for transfers between devices, shift_slot(): return lax.ppermute(value, ('blk', 'uly'), pairs)  5.47 us
  transfers between devices with their start and end apart: 4, of which 3 were waited for; matrix products, arithmetic and copies ran while one was open for 0% of the time, Pallas kernels for 21%

profile of v7, /device:TPU:64, one launch (start us, length us, event | category | flops | bytes accessed | tf_op | source)
XLA Modules:
  0.0 90.2 jit_solution(17185209687265471373)
XLA Ops:
  0.6 3.4 %pack_heads_0.1 = bf16[8,784,128]{2,1,0:T(8,128)(2,1)} custom-call(bf16[128,4096]{1,0:T(8,128)(2,1)} %refs_0_.3, bf16[128,4096]{1,0:T(8,128)(2,1)} %refs_1_.3, bf16[128,4096]{1,0:T(8,128)(2,1)} %refs_2_.3, f32[32,128]{1,0:T(8,128)} %bitcast.6, bf16[128,1024]{1,0:T(8,128)(2,1)} %refs_4_.1, bf16[128,1024]{1,0:T(8,128)(2,1)} %refs_5_.1), custom_call_target="tpu_custom_call" | custom-call | flops 671088640 | bytes 1048576 | tf_op jit(solution)/shard_map/pack_heads_0/pallas_call | solution.py:432
  4.0 5.5 %all-to-all-start = ((bf16[8,784,128]{2,1,0:T(8,128)(2,1)}), bf16[8,784,128]{2,1,0:T(8,128)(2,1)S(1)}, u32[]{:S(2)}, u32[]{:S(2)}) async-start(bf16[8,784,128]{2,1,0:T(8,128)(2,1)} %pack_heads_0.1), calls=%async_computation | async-start | bytes 3211264 | tf_op jit(solution)/shard_map/all_to_all | solution.py:420
  9.6 3.4 %pack_heads_2.1 = bf16[8,528,128]{2,1,0:T(8,128)(2,1)} custom-call(bf16[128,4096]{1,0:T(8,128)(2,1)} %refs_0_.3, bf16[128,4096]{1,0:T(8,128)(2,1)} %refs_1_.3, bf16[128,4096]{1,0:T(8,128)(2,1)} %refs_2_.3, f32[32,128]{1,0:T(8,128)} %bitcast.7), custom_call_target="tpu_custom_call" | custom-call | flops 671088640 | bytes 1048576 | tf_op jit(solution)/shard_map/pack_heads_2/pallas_call | solution.py:432
  13.0 17.8 %all-to-all-done.x_ref.x0_ref = bf16[8,784,128]{2,1,0:T(8,128)(2,1)S(1)} async-done(((bf16[8,784,128]{2,1,0:T(8,128)(2,1)}), bf16[8,784,128]{2,1,0:T(8,128)(2,1)S(1)}, u32[]{:S(2)}, u32[]{:S(2)}) %all-to-all-start) | async-done | bytes 1605664 | tf_op jit(solution)/shard_map/all_to_all | solution.py:420
  30.8 3.6 %all-to-all-start.1 = ((bf16[8,528,128]{2,1,0:T(8,128)(2,1)}), bf16[8,528,128]{2,1,0:T(8,128)(2,1)S(1)}, u32[]{:S(2)}, u32[]{:S(2)}) async-start(bf16[8,528,128]{2,1,0:T(8,128)(2,1)} %pack_heads_2.1), calls=%async_computation.1 | async-start | bytes 2162688 | tf_op jit(solution)/shard_map/all_to_all | solution.py:420
  34.3 0.0 copy-start
  34.4 0.8 collective-permute-start
  35.2 0.0 copy-done
  35.2 5.2 %local_first.1 = (f32[2,8,128,128]{3,2,1,0:T(8,128)S(1)}, f32[2,8,128,128]{3,2,1,0:T(8,128)}) custom-call(s32[2,16]{1,0:T(2,128)S(1)} %bitcast.2, bf16[8,784,128]{2,1,0:T(8,128)(2,1)S(1)} %all-to-all-done.x_ref.x0_ref), custom_call_target="tpu_custom_call" | custom-call | flops 4026531840 | bytes 4194304 | tf_op jit(solution)/shard_map/local_first/pallas_call | solution.py:432
  40.4 4.8 %collective-permute-done.kp_ref = bf16[8,256,128]{2,1,0:T(8,128)(2,1)S(1)} collective-permute-done((bf16[8,256,128]{2,1,0:T(8,128)(2,1)S(1)}, bf16[8,256,128]{2,1,0:T(8,128)(2,1)S(1)}, u32[]{:S(2)}, u32[]{:S(2)}) %collective-permute-start) | collective-permute-done | bytes 524320 | tf_op jit(solution)/shard_map/ppermute | solution.py:415
  45.2 4.6 %cross_first.1 = (bf16[8,768,128]{2,1,0:T(8,128)(2,1)}, f32[2,8,128,128]{3,2,1,0:T(8,128)}) custom-call(s32[2,16]{1,0:T(2,128)S(1)} %bitcast.3, bf16[8,784,128]{2,1,0:T(8,128)(2,1)S(1)} %all-to-all-done.x_ref.x0_ref, bf16[8,256,128]{2,1,0:T(8,128)(2,1)S(1)} %collective-permute-done.kp_ref, f32[2,8,128,128]{3,2,1,0:T(8,128)S(1)} %get-tuple-element.15.dq_in), custom_call_target="tpu_custom_call" | custom-call | flops 2684354560 | bytes 4194304 | tf_op jit(solution)/shard_map/cross_first/pallas_call | solution.py:432
  49.8 0.0 all-to-all-done.1.x_ref
  49.8 4.0 %cross_last.1 = (bf16[2,512,1024]{2,1,0:T(8,128)(2,1)S(1)}, bf16[2,8,128,128]{3,2,1,0:T(8,128)(2,1)S(1)}) custom-call(s32[2,16]{1,0:T(2,128)S(1)} %bitcast.4, bf16[8,528,128]{2,1,0:T(8,128)(2,1)S(1)} %all-to-all-done.1.x_ref, bf16[8,256,128]{2,1,0:T(8,128)(2,1)S(1)} %collective-permute-done.kp_ref, f32[2,8,128,128]{3,2,1,0:T(8,128)} %get-tuple-element.16.cross_hbm), custom_call_target="tpu_custom_call" | custom-call | flops 2684354560 | bytes 4194304 | tf_op jit(solution)/shard_map/cross_last/pallas_call | solution.py:432
  53.8 0.3 collective-permute-start.1
  54.1 6.0 %local_last.1 = (bf16[8,768,128]{2,1,0:T(8,128)(2,1)}, f32[2,8,128,128]{3,2,1,0:T(8,128)S(1)}) custom-call(s32[2,16]{1,0:T(2,128)S(1)} %bitcast.5, bf16[8,528,128]{2,1,0:T(8,128)(2,1)S(1)} %all-to-all-done.1.x_ref, bf16[8,784,128]{2,1,0:T(8,128)(2,1)S(1)} %all-to-all-done.x_ref.x0_ref, ...), custom_call_target="tpu_custom_call", output_to_operand_aliasing={{0}: (6, {})} | custom-call | flops 4026531840 | bytes 4194304 | tf_op jit(solution)/shard_map/local_last/pallas_call | solution.py:432
  60.1 0.7 collective-permute-done.1.back_ref
  60.8 0.9 add_returned.1
  61.7 27.2 %all_to_all.15.x_ref = bf16[8,768,128]{2,1,0:T(8,128)(2,1)S(1)} all-to-all(bf16[8,768,128]{2,1,0:T(8,128)(2,1)} %add_returned.1), channel_id=1, replica_groups={{0,2,4,6,1,3,5,7},{15,12,11,8,14,13,10,9},{16,18,20,22,17,19,21,23},{31..., dimensions={0} | all-to-all | bytes 3145728 | tf_op jit(solution)/shard_map/all_to_all | solution.py:420
  88.9 1.1 %unpack.1 = (bf16[128,4096]{1,0:T(8,128)(2,1)}, bf16[128,1024]{1,0:T(8,128)(2,1)}, bf16[128,1024]{1,0:T(8,128)(2,1)}) custom-call(bf16[8,768,128]{2,1,0:T(8,128)(2,1)S(1)} %all_to_all.15.x_ref), custom_call_target="tpu_custom_call" | custom-call | tf_op jit(solution)/shard_map/unpack/pallas_call | solution.py:432
  (1 shorter events, 0.0 us)
Async XLA Ops:
  4.0 26.7 %all-to-all-start = ((bf16[8,784,128]{2,1,0:T(8,128)(2,1)}), bf16[8,784,128]{2,1,0:T(8,128)(2,1)S(1)}, u32[]{:S(2)}, u32[]{:S(2)}) async-start(bf16[8,784,128]{2,1,0:T(8,128)(2,1)} %pack_heads_0.1), calls=%async_computation | async-start | bytes 3211264 | tf_op jit(solution)/shard_map/all_to_all | solution.py:420
  30.8 19.0 %all-to-all-start.1 = ((bf16[8,528,128]{2,1,0:T(8,128)(2,1)}), bf16[8,528,128]{2,1,0:T(8,128)(2,1)S(1)}, u32[]{:S(2)}, u32[]{:S(2)}) async-start(bf16[8,528,128]{2,1,0:T(8,128)(2,1)} %pack_heads_2.1), calls=%async_computation.1 | async-start | bytes 2162688 | tf_op jit(solution)/shard_map/all_to_all | solution.py:420
  34.3 0.8 copy-start
  34.4 10.8 %collective-permute-start = (bf16[8,256,128]{2,1,0:T(8,128)(2,1)S(1)}, bf16[8,256,128]{2,1,0:T(8,128)(2,1)S(1)}, u32[]{:S(2)}, u32[]{:S(2)}) collective-permute-start(bf16[8,256,128]{2,1,0:T(8,128)(2,1)S(1)} %take_keys.1), channel_id=1, source_target_pairs={{0,8},{1,9},{2,10},{3,11},{4,12},{5,13},{6,14},{7,15},{8,16},{9,17... | collective-permute-start | bytes 1572872 | tf_op jit(solution)/shard_map/ppermute | solution.py:415
  53.8 7.0 %collective-permute-start.1 = (bf16[2,8,128,128]{3,2,1,0:T(8,128)(2,1)S(1)}, bf16[2,8,128,128]{3,2,1,0:T(8,128)(2,1)S(1)}, u32[]{:S(2)}, u32[]{:S(2)}) collective-permute-start(bf16[2,8,128,128]{3,2,1,0:T(8,128)(2,1)S(1)} %get-tuple-element.21), channel_id=1, source_target_pairs={{0,121},{1,120},{2,123},{3,122},{4,125},{5,124},{6,127},{7,126},{8... | collective-permute-start | bytes 1572872 | tf_op jit(solution)/shard_map/ppermute | solution.py:415
